TPU v7x, 32 devices: a whole 2x2x4 slice. The times are simulated.
32 devices in a mesh: exp: 16 (over z, x, core), tp: 2 (over y).
Axes of the slice: x: 2, y: 2, z: 4, core: 2. Of those that a mesh axis runs over, the one named last changes fastest.
Arguments:
- tokens: bfloat16 [8192, 1024], P(('exp', 'tp')), may hold values from -6 to 6
- gain_attn: float32 [1024], replicated, may hold values from 0.1 to 1.9
- w_query: bfloat16 [1024, 1024], P(None, 'tp'), may hold values from -0.25 to 0.25
- w_key: bfloat16 [1024, 512], P(None, 'tp'), may hold values from -0.25 to 0.25
- w_value: bfloat16 [1024, 512], P(None, 'tp'), may hold values from -0.1875 to 0.1875
- w_out: bfloat16 [1024, 1024], replicated, may hold values from -0.5 to 0.5
- gain_ffn: float32 [1024], replicated, may hold values from 0.1 to 1.9
- w_router: bfloat16 [1024, 32], replicated, may hold values from -0.09375 to 0.09375
- w_gate: bfloat16 [32, 1024, 512], P('exp', None, 'tp'), may hold values from -0.1875 to 0.1875
- w_up: bfloat16 [32, 1024, 512], P('exp', None, 'tp'), may hold values from -0.1875 to 0.1875
- w_down: bfloat16 [32, 512, 1024], P('exp', 'tp'), may hold values from -1 to 1
- segment_ids: int32 [8192], P('exp'), may hold values from 0 to 15, never falling along the last dimension, each value on 1 to 2000 neighbouring positions
- routes: int32 [8192, 8], P(('exp', 'tp')), may hold values from 0 to 31, all different within a row; in each aligned block of 256 rows (0 to 255, 256 to 511, ...) at most 128 rows name the same one
- out_grad: bfloat16 [8192, 1024], P(('exp', 'tp')), may hold values from -6 to 6
Outputs:
- output: bfloat16 [8192, 1024], P(('exp', 'tp'))
- input_grad: float32 [8192, 1024], P(('exp', 'tp'))
- gain_attn_grad: float32 [1024], replicated
- w_query_grad: float32 [1024, 1024], P(None, 'tp')
- w_key_grad: float32 [1024, 512], P(None, 'tp')
- w_value_grad: float32 [1024, 512], P(None, 'tp')
- w_out_grad: float32 [1024, 1024], replicated
- gain_ffn_grad: float32 [1024], replicated
- w_router_grad: float32 [1024, 32], replicated
- w_gate_grad: float32 [32, 1024, 512], P('exp', None, 'tp')
- w_up_grad: float32 [32, 1024, 512], P('exp', None, 'tp')
- w_down_grad: float32 [32, 512, 1024], P('exp', 'tp')
Inputs may be any that keep to these rules, and one draw needn't show every extreme that they name: `routes`: each row names 8 different experts. In the rows of one device (aligned blocks of 256 rows) each expert is named by at most 128 rows, a bound that some block reaches. `segment_ids`: never falling along the array; each document number covers 1 to 2000 consecutive tokens, one exactly 2000.
All inputs are finite; a program needn't handle non-finite values.
Results may differ from a plain program's by a relative error of at most 0.023.
Values may be sent and summed in bfloat16 or wider, within the bound.
A program may use at most 192 MiB of HBM per device.

v0:
```python
import jax
import jax.numpy as jnp
from jax import lax
from jax.sharding import PartitionSpec as P

HEAD = 64
SEQ_LEN = 512
CAP = 128


epsilon = 1e-06
base_theta = 10000.0


def contract(left, right, left_dim, right_dim):
    return lax.dot_general(
        left, right, (((left_dim,), (right_dim,)), ((), ())), preferred_element_type=jnp.float32
    )


def doc_positions(seg_rows):
    indices = jnp.arange(seg_rows.shape[-1], dtype=jnp.int32)
    previous = jnp.concatenate([seg_rows[..., :1], seg_rows[..., :-1]], axis=-1)
    starts = (indices == 0) | (seg_rows != previous)
    latest = lax.cummax(jnp.where(starts, indices, 0), axis=seg_rows.ndim - 1)
    return indices - latest


def rope_tables(positions, head_dim):
    halves = head_dim // 2
    frequency = base_theta ** (-2.0 * jnp.arange(halves, dtype=jnp.float32) / head_dim)
    angles = positions.astype(jnp.float32)[:, None] * frequency[None, :]
    angles = jnp.concatenate([angles, angles], axis=1)
    return (jnp.cos(angles)[:, None, :], jnp.sin(angles)[:, None, :])


def rotate(values, cos_table, sin_table):
    halves = values.shape[-1] // 2
    turned = jnp.concatenate([-values[..., halves:], values[..., :halves]], axis=-1)
    return values * cos_table + turned * sin_table


def rotate_back(grads, cos_table, sin_table):
    halves = grads.shape[-1] // 2
    scaled = grads * sin_table
    return grads * cos_table + jnp.concatenate(
        [scaled[..., halves:], -scaled[..., :halves]], axis=-1
    )


def masked_scores(queries, key_rows, seg_rows):
    length, kv_heads, head_dim = key_rows.shape
    grouped = queries.reshape(length, kv_heads, -1, head_dim)
    raw_scores = jnp.einsum(
        "qhgd,khd->hgqk", grouped, key_rows, preferred_element_type=jnp.float32
    ) * head_dim ** (-0.5)
    indices = jnp.arange(length)
    allowed = (indices[:, None] >= indices[None, :]) & (seg_rows[:, None] == seg_rows[None, :])
    return (jnp.where(allowed, raw_scores, -1e30), grouped)


def attend_forward(seq_item):
    queries, key_rows, value_rows, seg_rows = seq_item
    scores, grouped = masked_scores(queries, key_rows, seg_rows)
    highest = jnp.max(scores, axis=-1, keepdims=True)
    weights = jnp.exp(scores - highest)
    totals = jnp.sum(weights, axis=-1, keepdims=True)
    shares = (weights / totals).astype(jnp.bfloat16)
    attended = jnp.einsum("hgqk,khd->qhgd", shares, value_rows, preferred_element_type=jnp.float32)
    return (attended.reshape(queries.shape[0], -1), highest + jnp.log(totals))


def attend_backward(seq_item):
    queries, key_rows, value_rows, seg_rows, log_total, head_grad = seq_item
    scores, grouped = masked_scores(queries, key_rows, seg_rows)
    factor = key_rows.shape[2] ** (-0.5)
    shares = jnp.exp(scores - log_total)
    grad_grouped = head_grad.reshape(grouped.shape)
    share_grad = jnp.einsum(
        "qhgd,khd->hgqk", grad_grouped, value_rows, preferred_element_type=jnp.float32
    )
    row_dot = jnp.sum(shares * share_grad, axis=-1, keepdims=True)
    score_grad = (shares * (share_grad - row_dot)).astype(jnp.bfloat16)
    query_grad = (
        jnp.einsum("hgqk,khd->qhgd", score_grad, key_rows, preferred_element_type=jnp.float32)
        * factor
    )
    key_grad = (
        jnp.einsum("hgqk,qhgd->khd", score_grad, grouped, preferred_element_type=jnp.float32)
        * factor
    )
    value_grad = jnp.einsum(
        "hgqk,qhgd->khd",
        shares.astype(jnp.bfloat16),
        grad_grouped,
        preferred_element_type=jnp.float32,
    )
    return (query_grad.reshape(queries.shape[0], -1), key_grad, value_grad)


def shards(
    tokens,
    gain_attn,
    w_query,
    w_key,
    w_value,
    w_out,
    gain_ffn,
    w_router,
    w_gate,
    w_up,
    w_down,
    segment_ids,
    routes,
    out_grad,
):
    tok_rows, width = tokens.shape
    group_rows = segment_ids.shape[0]
    seq_len = SEQ_LEN
    seq_count = group_rows // seq_len
    query_cols = w_query.shape[1]
    kv_cols = w_key.shape[1]
    head_dim = HEAD
    tp_index = lax.axis_index("tp")
    expert_count = w_router.shape[1]
    capacity = CAP
    top_count = routes.shape[1]
    local_experts = w_gate.shape[0]
    owner_count = lax.axis_size("exp")
    gate_full, up_full, down_full = (
        lax.all_gather(w_gate, "tp", axis=2, tiled=True),
        lax.all_gather(w_up, "tp", axis=2, tiled=True),
        lax.all_gather(w_down, "tp", axis=1, tiled=True),
    )
    source = tokens.astype(jnp.float32)
    scale_one = lax.rsqrt(jnp.mean(source * source, axis=1, keepdims=True) + epsilon)
    unit_one = source * scale_one
    normed = (unit_one * gain_attn).astype(jnp.bfloat16)
    gathered = lax.all_gather(normed, "tp", axis=0, tiled=True)
    w_proj = jnp.concatenate([w_query, w_key, w_value], axis=1)
    projected = jnp.dot(gathered, w_proj, preferred_element_type=jnp.float32)
    seq_rows = segment_ids.reshape(seq_count, seq_len)
    cos_table, sin_table = rope_tables(doc_positions(seq_rows).reshape(-1), head_dim)
    queries = rotate(
        projected[:, :query_cols].reshape(group_rows, -1, head_dim), cos_table, sin_table
    ).astype(jnp.bfloat16)
    key_rows = rotate(
        projected[:, query_cols : query_cols + kv_cols].reshape(group_rows, -1, head_dim),
        cos_table,
        sin_table,
    ).astype(jnp.bfloat16)
    value_rows = (
        projected[:, query_cols + kv_cols :].astype(jnp.bfloat16).reshape(group_rows, -1, head_dim)
    )
    query_seqs = queries.reshape(seq_count, seq_len, -1, head_dim)
    key_seqs = key_rows.reshape(seq_count, seq_len, -1, head_dim)
    value_seqs = value_rows.reshape(seq_count, seq_len, -1, head_dim)
    attended, log_total = lax.map(attend_forward, (query_seqs, key_seqs, value_seqs, seq_rows))
    head_rows = attended.reshape(group_rows, query_cols).astype(jnp.bfloat16)
    out_local = lax.dynamic_slice_in_dim(w_out, tp_index * query_cols, query_cols, 0)
    part_rows = head_rows
    branch = lax.psum_scatter(
        jnp.dot(part_rows, out_local, preferred_element_type=jnp.float32),
        "tp",
        scatter_dimension=0,
        tiled=True,
    )
    hidden = source + branch
    scale_two = lax.rsqrt(jnp.mean(hidden * hidden, axis=1, keepdims=True) + epsilon)
    unit_two = hidden * scale_two
    normed_ffn = (unit_two * gain_ffn).astype(jnp.bfloat16)
    logits = jnp.dot(normed_ffn, w_router, preferred_element_type=jnp.float32)
    expert_ids = jnp.arange(expert_count, dtype=jnp.int32)
    route_hits = routes[:, :, None] == expert_ids[None, None, :]
    chosen = jnp.sum(jnp.where(route_hits, logits[:, None, :], 0.0), axis=2)
    highest = jnp.max(chosen, axis=1, keepdims=True)
    weights = jnp.exp(chosen - highest)
    gate_shares = weights / jnp.sum(weights, axis=1, keepdims=True)
    flat_routes = routes.reshape(-1)
    onehot = (flat_routes[:, None] == expert_ids[None, :]).astype(jnp.int32)
    rank_rows = jnp.sum((jnp.cumsum(onehot, axis=0) - onehot) * onehot, axis=1)
    slot_index = flat_routes * capacity + rank_rows
    route_count = tok_rows * top_count
    slot_total = expert_count * capacity
    route_of_slot = (
        jnp.zeros((slot_total,), jnp.int32)
        .at[slot_index]
        .set(jnp.arange(route_count, dtype=jnp.int32))
    )
    filled = jnp.zeros((slot_total,), jnp.int32).at[slot_index].set(1)
    empty_row = jnp.zeros((), jnp.bfloat16)
    packed = jnp.where(filled[:, None] > 0, normed_ffn[route_of_slot // top_count], empty_row)
    packed = packed.reshape(owner_count, local_experts, capacity, width)
    received = lax.all_to_all(packed, "exp", split_axis=0, concat_axis=0, tiled=True)
    gate_pre = jnp.einsum("sucd,udf->sucf", received, gate_full, preferred_element_type=jnp.float32)
    up_pre = jnp.einsum("sucd,udf->sucf", received, up_full, preferred_element_type=jnp.float32)
    inner_act = (gate_pre * jax.nn.sigmoid(gate_pre) * up_pre).astype(jnp.bfloat16)
    result = jnp.einsum(
        "sucf,ufd->sucd", inner_act, down_full, preferred_element_type=jnp.float32
    ).astype(jnp.bfloat16)
    returned = lax.all_to_all(result, "exp", split_axis=0, concat_axis=0, tiled=True)
    returned, received, gate_pre, up_pre = (returned, received, gate_pre, up_pre)
    slot_results = returned.reshape(slot_total, width)
    picked = slot_results[slot_index].reshape(tok_rows, top_count, width)
    mixture = jnp.sum(gate_shares[:, :, None] * picked.astype(jnp.float32), axis=1)
    output = (hidden + mixture).astype(jnp.bfloat16)
    share_grad = jnp.einsum("td,tkd->tk", out_grad, picked, preferred_element_type=jnp.float32)
    result_grad = (
        (gate_shares[:, :, None] * out_grad.astype(jnp.float32)[:, None, :])
        .astype(jnp.bfloat16)
        .reshape(route_count, width)
    )
    packed_grad = jnp.where(filled[:, None] > 0, result_grad[route_of_slot], empty_row)
    packed_grad = packed_grad.reshape(owner_count, local_experts, capacity, width)
    arrived = lax.all_to_all(packed_grad, "exp", split_axis=0, concat_axis=0, tiled=True)
    sigmoid_gate = jax.nn.sigmoid(gate_pre)
    inner_act = (gate_pre * sigmoid_gate * up_pre).astype(jnp.bfloat16)
    inner_grad = jnp.einsum(
        "sucd,ufd->sucf", arrived, down_full, preferred_element_type=jnp.float32
    )
    down_part = jnp.einsum("sucf,sucd->ufd", inner_act, arrived, preferred_element_type=jnp.float32)
    gate_grad = (
        inner_grad * up_pre * sigmoid_gate * (1.0 + gate_pre * (1.0 - sigmoid_gate))
    ).astype(jnp.bfloat16)
    up_grad = (inner_grad * gate_pre * sigmoid_gate).astype(jnp.bfloat16)
    back_rows = (
        jnp.einsum("sucf,udf->sucd", gate_grad, gate_full, preferred_element_type=jnp.float32)
        + jnp.einsum("sucf,udf->sucd", up_grad, up_full, preferred_element_type=jnp.float32)
    ).astype(jnp.bfloat16)
    gate_part = jnp.einsum(
        "sucd,sucf->udf", received, gate_grad, preferred_element_type=jnp.float32
    )
    up_part = jnp.einsum("sucd,sucf->udf", received, up_grad, preferred_element_type=jnp.float32)
    slot_grads = lax.all_to_all(back_rows, "exp", split_axis=0, concat_axis=0, tiled=True).reshape(
        slot_total, width
    )
    ffn_grad = jnp.sum(
        slot_grads[slot_index].reshape(tok_rows, top_count, width).astype(jnp.float32), axis=1
    )
    mixed_grad = gate_shares * (
        share_grad - jnp.sum(gate_shares * share_grad, axis=1, keepdims=True)
    )
    logit_grad = jnp.sum(jnp.where(route_hits, mixed_grad[:, :, None], 0.0), axis=1).astype(
        jnp.bfloat16
    )
    router_part = contract(normed_ffn, logit_grad, 0, 0)
    ffn_grad = ffn_grad + contract(logit_grad, w_router, 1, 1)
    ffn_part = jnp.sum(ffn_grad * unit_two, axis=0)
    unit_grad_two = ffn_grad * gain_ffn
    hidden_grad = out_grad.astype(jnp.float32) + scale_two * (
        unit_grad_two - unit_two * jnp.mean(unit_grad_two * unit_two, axis=1, keepdims=True)
    )
    branch_low = hidden_grad.astype(jnp.bfloat16)
    part_rows = lax.all_gather(branch_low, "tp", axis=0, tiled=True)
    update = contract(part_rows, out_local, 1, 1)
    grads_heads = update
    grads_heads, out_rows = (grads_heads, contract(head_rows, part_rows, 0, 0))
    head_grad = grads_heads.astype(jnp.bfloat16)
    out_part = lax.dynamic_update_slice_in_dim(
        jnp.zeros(w_out.shape, jnp.float32), out_rows, tp_index * query_cols, 0
    )
    query_grad, key_grad, value_grad = lax.map(
        attend_backward,
        (
            query_seqs,
            key_seqs,
            value_seqs,
            seq_rows,
            log_total,
            head_grad.reshape(seq_count, seq_len, query_cols),
        ),
    )
    query_grad = rotate_back(query_grad.reshape(group_rows, -1, head_dim), cos_table, sin_table)
    key_grad = rotate_back(key_grad.reshape(group_rows, -1, head_dim), cos_table, sin_table)
    proj_grad = jnp.concatenate(
        [
            query_grad.reshape(group_rows, -1),
            key_grad.reshape(group_rows, -1),
            value_grad.reshape(group_rows, -1),
        ],
        axis=1,
    ).astype(jnp.bfloat16)
    proj_part = contract(gathered, proj_grad, 0, 0)
    part_rows = proj_grad
    normed_grad = lax.psum_scatter(
        contract(part_rows, w_proj, 1, 1).astype(jnp.bfloat16),
        "tp",
        scatter_dimension=0,
        tiled=True,
    ).astype(jnp.float32)
    attn_part = jnp.sum(normed_grad * unit_one, axis=0)
    unit_grad_one = normed_grad * gain_attn
    input_grad = hidden_grad + scale_one * (
        unit_grad_one - unit_one * jnp.mean(unit_grad_one * unit_one, axis=1, keepdims=True)
    )
    gate_weight_grad, up_weight_grad, down_weight_grad = (
        lax.psum_scatter(
            gate_part.astype(jnp.bfloat16), "tp", scatter_dimension=2, tiled=True
        ).astype(jnp.float32),
        lax.psum_scatter(
            up_part.astype(jnp.bfloat16), "tp", scatter_dimension=2, tiled=True
        ).astype(jnp.float32),
        lax.psum_scatter(
            down_part.astype(jnp.bfloat16), "tp", scatter_dimension=1, tiled=True
        ).astype(jnp.float32),
    )
    query_weight_grad, key_weight_grad, value_weight_grad = (
        lax.psum(proj_part[:, :query_cols].astype(jnp.bfloat16), "exp").astype(jnp.float32),
        lax.psum(
            proj_part[:, query_cols : query_cols + kv_cols].astype(jnp.bfloat16), "exp"
        ).astype(jnp.float32),
        lax.psum(proj_part[:, query_cols + kv_cols :].astype(jnp.bfloat16), "exp").astype(
            jnp.float32
        ),
    )
    attn_gain_grad, ffn_gain_grad, router_grad, out_weight_grad = lax.psum(
        (attn_part, ffn_part, router_part, out_part), ("exp", "tp")
    )
    return (
        output,
        input_grad,
        attn_gain_grad,
        query_weight_grad,
        key_weight_grad,
        value_weight_grad,
        out_weight_grad,
        ffn_gain_grad,
        router_grad,
        gate_weight_grad,
        up_weight_grad,
        down_weight_grad,
    )


def solution(mesh):
    in_specs = (
        P(("exp", "tp"), None),
        P(),
        P(None, "tp"),
        P(None, "tp"),
        P(None, "tp"),
        P(),
        P(),
        P(),
        P("exp", None, "tp"),
        P("exp", None, "tp"),
        P("exp", "tp", None),
        P("exp"),
        P(("exp", "tp"), None),
        P(("exp", "tp"), None),
    )
    out_specs = (
        P(("exp", "tp"), None),
        P(("exp", "tp"), None),
        P(),
        P(None, "tp"),
        P(None, "tp"),
        P(None, "tp"),
        P(),
        P(),
        P(),
        P("exp", None, "tp"),
        P("exp", None, "tp"),
        P("exp", "tp", None),
    )
    return jax.shard_map(shards, mesh=mesh, in_specs=in_specs, out_specs=out_specs, check_vma=False)
```

profile of v0, /device:TPU:0, one launch (start us, length us, event | category | flops | bytes accessed | tf_op | source)
XLA Modules:
  0.0 1459.3 jit_solution(1912329780485906546)
XLA Ops:
  19.5 15.4 %all-gather.6.cloned.1.call-done = bf16[512,1024]{1,0:T(8,128)(2,1)} async-done(((bf16[256,1024]{1,0:T(8,128)(2,1)}), bf16[512,1024]{1,0:T(8,128)(2,1)}) %all-gather.6.cloned.1.call-update) | async-done | bytes 1048592 | tf_op jit(solution)/shard_map/all_gather | solution.py:139
  91.2 18.2 %gather_fusion = bf16[4096,1024]{1,0:T(8,128)(2,1)} fusion(bf16[256,1024]{1,0:T(8,128)(2,1)S(1)} %multiply_convert_fusion, s32[4096]{0:T(1024)S(1)} %get-tuple-element.97), kind=kCustom, calls=%fused_computation | custom fusion | bytes 16793600 | tf_op jit(solution)/shard_map/gather | solution.py:192
  124.2 34.0 %all-gather.8.cloned.1.call-done = bf16[2,1024,512]{2,1,0:T(8,128)(2,1)} async-done(((bf16[2,1024,256]{2,1,0:T(8,128)(2,1)}), bf16[2,1024,512]{2,1,0:T(8,128)(2,1)}) %all-gather.8.cloned.1.call-update) | async-done | bytes 2097168 | tf_op jit(solution)/shard_map/all_gather | solution.py:131
  158.2 114.8 %all-to-all-done = bf16[16,2,128,1024]{3,2,1,0:T(8,128)(2,1)} async-done(((bf16[16,2,128,1024]{3,2,1,0:T(8,128)(2,1)}), bf16[16,2,128,1024]{3,2,1,0:T(8,128)(2,1)}, u32[]{:S(2)}, u32[]{:S(2)}) %all-to-all-start) | async-done | bytes 8388640 | tf_op jit(solution)/shard_map/all_to_all | solution.py:194
  273.0 11.8 fusion.22
  284.8 12.3 fusion.10
  297.1 10.6 convert_bitcast_fusion
  315.9 48.4 %all-to-all-start.1 = ((bf16[16,2,128,1024]{3,2,1,0:T(8,128)(2,1)}), bf16[16,2,128,1024]{3,2,1,0:T(8,128)(2,1)}, u32[]{:S(2)}, u32[]{:S(2)}) async-start(bf16[16,2,128,1024]{3,2,1,0:T(8,128)(2,1)} %copy.103), calls=%async_computation.2 | async-start | bytes 16777216 | tf_op jit(solution)/shard_map/all_to_all | solution.py:201
  365.8 149.2 %all-to-all-done.1 = bf16[16,2,128,1024]{3,2,1,0:T(8,128)(2,1)} async-done(((bf16[16,2,128,1024]{3,2,1,0:T(8,128)(2,1)}), bf16[16,2,128,1024]{3,2,1,0:T(8,128)(2,1)}, u32[]{:S(2)}, u32[]{:S(2)}) %all-to-all-start.1) | async-done | bytes 8388640 | tf_op jit(solution)/shard_map/all_to_all | solution.py:201
  515.0 15.4 %gather_fusion.1 = bf16[2048,1024]{1,0:T(8,128)(2,1)} fusion(bf16[4096,1024]{1,0:T(8,128)(2,1)} %bitcast.35, s32[2048]{0:T(1024)S(1)} %broadcast_clamp_fusion), kind=kCustom, calls=%fused_computation.1 | custom fusion | bytes 8396800 | tf_op jit(solution)/shard_map/gather | solution.py:204
  538.6 23.5 %gather_fusion.2 = bf16[4096,1024]{1,0:T(8,128)(2,1)} fusion(bf16[2048,1024]{1,0:T(8,128)(2,1)} %fusion.9, s32[4096]{0:T(1024)S(1)} %get-tuple-element.96), kind=kCustom, calls=%fused_computation.2 | custom fusion | bytes 16793600 | tf_op jit(solution)/shard_map/gather | solution.py:213
  566.5 218.7 %all_to_all.20 = bf16[16,2,128,1024]{3,2,1,0:T(8,128)(2,1)} all-to-all(bf16[16,2,128,1024]{3,2,1,0:T(8,128)(2,1)S(1)} %broadcast_select_fusion), channel_id=1, replica_groups=mesh['exp'=16,'tp'=2] {'exp'}, dimensions={0} | all-to-all | bytes 16777216 | tf_op jit(solution)/shard_map/all_to_all | solution.py:215
  785.2 16.0 %fusion.8 = (bf16[16,2,128,512]{3,2,0,1:T(8,128)(2,1)}, bf16[16,2,128,512]{3,2,0,1:T(8,128)(2,1)}) fusion(f32[2,16,128,512]{3,2,1,0:T(8,128)} %fusion.22, f32[2,16,128,512]{3,2,1,0:T(8,128)} %get-tuple-element.101, bf16[2,512,1024]{2,1,0:T(8,128)(2,1)S(1)} %copy-done.47, bf16[16,2,128,1024]{3,2,1,0:T(8,128)(2,1)} %all_to_all.20), kind=kOutput, calls=%fused_computation.20 | convolution fusion | flops 4322230272 | bytes 35651584 | tf_op jit(solution)/shard_map/sucd,ufd->sucf/dot_general | solution.py:218
  811.5 15.4 %fusion = bf16[16,2,128,1024]{3,2,0,1:T(8,128)(2,1)} fusion(f32[2,16,128,1024]{3,2,1,0:T(8,128)} %fusion.39, bf16[16,2,128,512]{3,2,0,1:T(8,128)(2,1)} %get-tuple-element.78, bf16[2,1024,512]{2,1,0:T(8,128)(2,1)} %all-gather.10.cloned.1.call-done), kind=kOutput, calls=%fused_computation.7 | convolution fusion | flops 4303355904 | bytes 31457280 | tf_op jit(solution)/shard_map/sucf,udf->sucd/dot_general | solution.py:228
  841.1 150.4 %all-to-all-done.3 = bf16[16,2,128,1024]{3,2,1,0:T(8,128)(2,1)} async-done(((bf16[16,2,128,1024]{3,2,1,0:T(8,128)(2,1)}), bf16[16,2,128,1024]{3,2,1,0:T(8,128)(2,1)}, u32[]{:S(2)}, u32[]{:S(2)}) %all-to-all-start.3) | async-done | bytes 8388640 | tf_op jit(solution)/shard_map/all_to_all | solution.py:234
  991.5 15.4 %gather_fusion.3 = bf16[2048,1024]{1,0:T(8,128)(2,1)} fusion(bf16[4096,1024]{1,0:T(8,128)(2,1)} %bitcast.44, s32[2048]{0:T(1024)S(1)} %broadcast_clamp_fusion), kind=kCustom, calls=%fused_computation.3 | custom fusion | bytes 8396800 | tf_op jit(solution)/shard_map/gather | solution.py:238
  1015.3 10.5 bitcast_convert_fusion
  1047.5 20.1 %all-gather.14.cloned.1.call-done = bf16[512,1024]{1,0:T(8,128)(2,1)} async-done(((bf16[256,1024]{1,0:T(8,128)(2,1)}), bf16[512,1024]{1,0:T(8,128)(2,1)}) %all-gather.14.cloned.1.call-update) | async-done | bytes 1048592 | tf_op jit(solution)/shard_map/all_gather | solution.py:254
  1105.1 31.9 %reduce-scatter.12.cloned.1.call-done = bf16[2,1024,256]{2,1,0:T(8,128)(2,1)} async-done(((bf16[2,1024,512]{2,1,0:T(8,128)(2,1)}), bf16[2,1024,256]{2,1,0:T(8,128)(2,1)}) %reduce-scatter.12.cloned.1.call-update) | async-done | bytes 1048592 | tf_op jit(solution)/shard_map/reduce_scatter | solution.py:300
  1139.7 32.1 %reduce-scatter.10.cloned.1.call-done = bf16[2,1024,256]{2,1,0:T(8,128)(2,1)} async-done(((bf16[2,1024,512]{2,1,0:T(8,128)(2,1)}), bf16[2,1024,256]{2,1,0:T(8,128)(2,1)}) %reduce-scatter.10.cloned.1.call-update) | async-done | bytes 1048592 | tf_op jit(solution)/shard_map/reduce_scatter | solution.py:297
  1174.5 99.7 %all-reduce.8.cloned.1.call-done = (bf16[1024,512]{1,0:T(8,128)(2,1)}, bf16[1024,256]{1,0:T(8,128)(2,1)}, bf16[1024,256]{1,0:T(8,128)(2,1)}) async-done(((bf16[1024,512]{1,0:T(8,128)(2,1)}, bf16[1024,256]{1,0:T(8,128)(2,1)}, bf16[1024,256]{1,0:T(8,128)(2,1)}), (bf16[1024,512]{1,0:T(8,128)(2,1)}, bf16[1024,256]{1,0:T(8,128)(2,1)}, bf16[1024,256]{1,0:T(8,128)(2,1)})) %all-reduce.8.cloned.1.call-update) | async-done | bytes 2097168 | tf_op jit(solution)/shard_map/psum | solution.py:308
  1280.2 16.2 %reduce-scatter.8.cloned.1.call-done = bf16[256,1024]{1,0:T(8,128)(2,1)} async-done(((bf16[512,1024]{1,0:T(8,128)(2,1)}), bf16[256,1024]{1,0:T(8,128)(2,1)}) %reduce-scatter.8.cloned.1.call-update) | async-done | bytes 524304 | tf_op jit(solution)/shard_map/reduce_scatter | solution.py:285
  1298.2 40.0 %all-reduce = (f32[1024]{0:T(1024)}, f32[1024]{0:T(1024)}) all-reduce(f32[1024]{0:T(1024)S(1)} %get-tuple-element.55, f32[1024]{0:T(1024)S(1)} %get-tuple-element.53), channel_id=1, replica_groups=mesh['exp'=16,'tp'=2] {'exp','tp'}, use_global_device_ids=true, to_apply=%region_24.25 | all-reduce | flops 2048 | bytes 16384 | tf_op jit(solution)/shard_map/psum | solution.py:316
  1341.9 104.9 %all-reduce.6.cloned.1.call-done = (f32[1024,1024]{1,0:T(8,128)}, f32[1024,32]{0,1:T(8,128)}) async-done(((f32[1024,1024]{1,0:T(8,128)}, f32[1024,32]{0,1:T(8,128)}), (f32[1024,1024]{1,0:T(8,128)}, f32[1024,32]{0,1:T(8,128)})) %all-reduce.6.cloned.1.call-update) | async-done | bytes 4325392 | tf_op jit(solution)/shard_map/psum | solution.py:316
  (247 shorter events, 219.2 us)
Async XLA Ops:
  7.2 47.3 %copy-start = (bf16[1024,1024]{1,0:T(8,128)(2,1)S(1)}, bf16[1024,1024]{1,0:T(8,128)(2,1)}, u32[]{:S(2)}) copy-start(bf16[1024,1024]{1,0:T(8,128)(2,1)} %param.19) | copy-start | bytes 6291460
  7.2 27.7 %all-gather.6.cloned.1.call-start = ((), (), s32[]{:S(2)}) async-start(), calls=%async_computation.9 | async-start | bytes 1572864 | tf_op jit(solution)/shard_map/all_gather | solution.py:139
  10.7 77.9 %reduce-scatter.6.cloned.1.call-start = ((), (), s32[]{:S(2)}) async-start(), calls=%async_computation.10 | async-start | bytes 3145728 | tf_op jit(solution)/shard_map/reduce_scatter | solution.py:162
  56.6 34.4 %copy-start.38 = (f32[1024]{0:T(1024)S(1)}, f32[1024]{0:T(1024)}, u32[]{:S(2)}) copy-start(f32[1024]{0:T(1024)} %param.20) | copy-start | bytes 12292
  91.2 274.2 %copy-start.1 = (bf16[256,1024]{1,0:T(8,128)(2,1)}, bf16[256,1024]{1,0:T(8,128)(2,1)S(1)}, u32[]{:S(2)}) copy-start(bf16[256,1024]{1,0:T(8,128)(2,1)S(1)} %multiply_convert_fusion) | copy-start | bytes 1572868
  116.6 156.4 %all-to-all-start = ((bf16[16,2,128,1024]{3,2,1,0:T(8,128)(2,1)}), bf16[16,2,128,1024]{3,2,1,0:T(8,128)(2,1)}, u32[]{:S(2)}, u32[]{:S(2)}) async-start(bf16[16,2,128,1024]{3,2,1,0:T(8,128)(2,1)} %broadcast_select_fusion.1), calls=%async_computation.1 | async-start | bytes 16777216 | tf_op jit(solution)/shard_map/all_to_all | solution.py:194
  122.3 35.9 %all-gather.8.cloned.1.call-start = ((), (), s32[]{:S(2)}) async-start(), calls=%async_computation.11 | async-start | bytes 3145728 | tf_op jit(solution)/shard_map/all_gather | solution.py:131
  123.1 161.7 %all-gather.10.cloned.1.call-start = ((), (), s32[]{:S(2)}) async-start(), calls=%async_computation.12 | async-start | bytes 3145728 | tf_op jit(solution)/shard_map/all_gather | solution.py:132
  123.6 173.5 %all-gather.12.cloned.1.call-start = ((), (), s32[]{:S(2)}) async-start(), calls=%async_computation.13 | async-start | bytes 3145728 | tf_op jit(solution)/shard_map/all_gather | solution.py:133
  315.9 48.4 %copy-start.11 = (bf16[256,1024]{1,0:T(8,128)(2,1)S(1)}, bf16[256,1024]{1,0:T(8,128)(2,1)}, u32[]{:S(2)}) copy-start(bf16[256,1024]{1,0:T(8,128)(2,1)} %param.27) | copy-start | bytes 1572868
  315.9 49.5 %copy-start.30 = (bf16[1024,32]{0,1:T(8,128)(2,1)S(1)}, bf16[1024,32]{0,1:T(8,128)(2,1)}, u32[]{:S(2)}) copy-start(bf16[1024,32]{0,1:T(8,128)(2,1)} %param.21) | copy-start | bytes 196612
  315.9 199.1 %all-to-all-start.1 = ((bf16[16,2,128,1024]{3,2,1,0:T(8,128)(2,1)}), bf16[16,2,128,1024]{3,2,1,0:T(8,128)(2,1)}, u32[]{:S(2)}, u32[]{:S(2)}) async-start(bf16[16,2,128,1024]{3,2,1,0:T(8,128)(2,1)} %copy.103), calls=%async_computation.2 | async-start | bytes 16777216 | tf_op jit(solution)/shard_map/all_to_all | solution.py:201
  566.5 218.7 %copy-start.47 = (bf16[2,512,1024]{2,1,0:T(8,128)(2,1)S(1)}, bf16[2,512,1024]{2,1,0:T(8,128)(2,1)}, u32[]{:S(2)}) copy-start(bf16[2,512,1024]{2,1,0:T(8,128)(2,1)} %all-gather.12.cloned.1.call-done) | copy-start | bytes 6291460
  835.1 156.4 %all-to-all-start.3 = ((bf16[16,2,128,1024]{3,2,1,0:T(8,128)(2,1)}), bf16[16,2,128,1024]{3,2,1,0:T(8,128)(2,1)}, u32[]{:S(2)}, u32[]{:S(2)}) async-start(bf16[16,2,128,1024]{3,2,1,0:T(8,128)(2,1)} %copy.106), calls=%async_computation.4 | async-start | bytes 16777216 | tf_op jit(solution)/shard_map/all_to_all | solution.py:234
  840.8 226.8 %all-gather.14.cloned.1.call-start = ((), (), s32[]{:S(2)}) async-start(), calls=%async_computation.14 | async-start | bytes 1572864 | tf_op jit(solution)/shard_map/all_gather | solution.py:254
  1015.2 87.1 %reduce-scatter.14.cloned.1.call-start = ((), (), s32[]{:S(2)}) async-start(), calls=%async_computation.18 | async-start | bytes 3145728 | tf_op jit(solution)/shard_map/reduce_scatter | solution.py:303
  1025.8 111.2 %reduce-scatter.12.cloned.1.call-start = ((), (), s32[]{:S(2)}) async-start(), calls=%async_computation.17 | async-start | bytes 3145728 | tf_op jit(solution)/shard_map/reduce_scatter | solution.py:300
  1036.7 135.1 %reduce-scatter.10.cloned.1.call-start = ((), (), s32[]{:S(2)}) async-start(), calls=%async_computation.16 | async-start | bytes 3145728 | tf_op jit(solution)/shard_map/reduce_scatter | solution.py:297
  1047.3 226.9 %all-reduce.8.cloned.1.call-start = ((), (), s32[]{:S(2)}) async-start(), calls=%async_computation.20 | async-start | bytes 4194304 | tf_op jit(solution)/shard_map/psum | solution.py:308
  1086.5 210.0 %reduce-scatter.8.cloned.1.call-start = ((), (), s32[]{:S(2)}) async-start(), calls=%async_computation.15 | async-start | bytes 1572864 | tf_op jit(solution)/shard_map/reduce_scatter | solution.py:285
  1090.5 356.2 %all-reduce.6.cloned.1.call-start = ((), (), s32[]{:S(2)}) async-start(), calls=%async_computation.19 | async-start | bytes 8650752 | tf_op jit(solution)/shard_map/psum | solution.py:316
  1139.7 156.8 %copy-start.40 = (f32[1024]{0:T(1024)S(1)}, f32[1024]{0:T(1024)}, u32[]{:S(2)}) copy-start(f32[1024]{0:T(1024)} %param.15) | copy-start | bytes 12292
  1139.7 156.8 %copy-start.45 = (f32[256]{0:T(256)S(1)}, f32[256]{0:T(256)}, u32[]{:S(2)}) copy-start(f32[256]{0:T(256)} %copy-done.44) | copy-start | bytes 3076
  1174.5 163.7 %copy-start.6 = (f32[256,1024]{1,0:T(8,128)S(1)}, f32[256,1024]{1,0:T(8,128)}, u32[]{:S(2)}) copy-start(f32[256,1024]{1,0:T(8,128)} %copy-done.4) | copy-start | bytes 3145732
  (42 other events, 296.6 us)
Sparse Core Ops, SparseCore 0:
  10.8 23.9 all-gather.5
  56.7 31.8 reduce-scatter.5
  124.8 33.4 all-gather.7
  159.7 33.0 all-gather.9
  194.3 33.1 all-gather.11
  1015.4 52.1 all-gather.13
  1070.5 31.8 reduce-scatter.13
  1105.2 31.8 reduce-scatter.11
  1139.9 31.8 reduce-scatter.9
  1176.1 98.0 all-reduce.7
  1276.6 19.8 reduce-scatter.7
  1303.1 143.5 all-reduce.5
where the time goes:
time: 1460 us
  waiting for transfers between devices  776 us (53%)
  blocking collectives  259 us (18%)
  matrix products  141 us (10%)
  local copies, waits for them, and re-layouts  134 us (9%)
  other arithmetic  73.4 us (5%)
  starting transfers between devices  61.5 us (4%)
  between operations  15.3 us (1%)
    all_to_all x1, blocking collectives, shards(): lax.all_to_all(packed_grad, 'exp', split_axis=0, concat_axis=0, tiled=True)  219 us
    all_to_all x1, waiting for transfers between devices, shards(): lax.all_to_all(back_rows, 'exp', split_axis=0, concat_axis=0, tiled=True)  150 us
    all_to_all x1, waiting for transfers between devices, shards(): lax.all_to_all(result, 'exp', split_axis=0, concat_axis=0, tiled=True)  149 us
    all_to_all x1, waiting for transfers between devices, shards(): lax.all_to_all(packed, 'exp', split_axis=0, concat_axis=0, tiled=True)  115 us
    psum x1, waiting for transfers between devices, shards(): lax.psum((attn_part, ffn_part, router_part, out_part), ('exp', 'tp'))  105 us
    psum x1, waiting for transfers between devices, shards(): lax.psum(proj_part[:, :query_cols].astype(jnp.bfloat16), 'exp')  99.7 us
    all_to_all x1, starting transfers between devices, shards(): lax.all_to_all(result, 'exp', split_axis=0, concat_axis=0, tiled=True)  48.4 us
    psum x1, blocking collectives, shards(): lax.psum((attn_part, ffn_part, router_part, out_part), ('exp', 'tp'))  40 us
  transfers between devices with their start and end apart: 15, of which 13 were waited for; matrix products, arithmetic and copies ran while one was open for 10% of the time, Pallas kernels for 0%

commit v1 on v0

--- a/solution.py
+++ b/solution.py
@@ -96,6 +96,13 @@
         preferred_element_type=jnp.float32,
     )
     return (query_grad.reshape(queries.shape[0], -1), key_grad, value_grad)
+
+
+def dense_gates(logits, routes, expert_ids):
+    hits = jnp.any(routes[:, :, None] == expert_ids[None, None, :], axis=1)
+    chosen = jnp.where(hits, logits, -jnp.inf)
+    weights = jnp.exp(chosen - jnp.max(chosen, axis=1, keepdims=True))
+    return weights / jnp.sum(weights, axis=1, keepdims=True)
 
 
 def shards(
@@ -132,6 +139,30 @@
         lax.all_gather(w_up, "tp", axis=2, tiled=True),
         lax.all_gather(w_down, "tp", axis=1, tiled=True),
     )
+    exp_index = lax.axis_index("exp")
+    routes_all = lax.all_gather(routes, "exp", axis=0, tiled=True)
+    og_all = lax.all_gather(out_grad, "exp", axis=0, tiled=True)
+    own_ids = exp_index * local_experts + jnp.arange(local_experts, dtype=jnp.int32)
+    own_hits = jnp.any(
+        routes_all.T.reshape(1, top_count, owner_count, tok_rows)
+        == own_ids[:, None, None, None],
+        axis=1,
+    )
+    tok_ids = jnp.arange(tok_rows, dtype=jnp.int32)
+    earlier = (tok_ids[:, None] < tok_ids[None, :]).astype(jnp.bfloat16)
+    ranks = jnp.einsum(
+        "usr,rt->ust", own_hits.astype(jnp.bfloat16), earlier, preferred_element_type=jnp.float32
+    ).astype(jnp.int32)
+    ranks = jnp.where(own_hits, ranks, -1)
+    dispatch = (
+        ranks[:, :, None, :] == jnp.arange(capacity, dtype=jnp.int32)[None, None, :, None]
+    ).astype(jnp.bfloat16)
+    og_packed = jnp.einsum(
+        "usct,std->uscd",
+        dispatch,
+        og_all.reshape(owner_count, tok_rows, width),
+        preferred_element_type=jnp.float32,
+    ).astype(jnp.bfloat16).reshape(local_experts, -1, width)
     source = tokens.astype(jnp.float32)
     scale_one = lax.rsqrt(jnp.mean(source * source, axis=1, keepdims=True) + epsilon)
     unit_one = source * scale_one
@@ -171,78 +202,76 @@
     normed_ffn = (unit_two * gain_ffn).astype(jnp.bfloat16)
     logits = jnp.dot(normed_ffn, w_router, preferred_element_type=jnp.float32)
     expert_ids = jnp.arange(expert_count, dtype=jnp.int32)
-    route_hits = routes[:, :, None] == expert_ids[None, None, :]
-    chosen = jnp.sum(jnp.where(route_hits, logits[:, None, :], 0.0), axis=2)
-    highest = jnp.max(chosen, axis=1, keepdims=True)
-    weights = jnp.exp(chosen - highest)
-    gate_shares = weights / jnp.sum(weights, axis=1, keepdims=True)
-    flat_routes = routes.reshape(-1)
-    onehot = (flat_routes[:, None] == expert_ids[None, :]).astype(jnp.int32)
-    rank_rows = jnp.sum((jnp.cumsum(onehot, axis=0) - onehot) * onehot, axis=1)
-    slot_index = flat_routes * capacity + rank_rows
-    route_count = tok_rows * top_count
-    slot_total = expert_count * capacity
-    route_of_slot = (
-        jnp.zeros((slot_total,), jnp.int32)
-        .at[slot_index]
-        .set(jnp.arange(route_count, dtype=jnp.int32))
-    )
-    filled = jnp.zeros((slot_total,), jnp.int32).at[slot_index].set(1)
-    empty_row = jnp.zeros((), jnp.bfloat16)
-    packed = jnp.where(filled[:, None] > 0, normed_ffn[route_of_slot // top_count], empty_row)
-    packed = packed.reshape(owner_count, local_experts, capacity, width)
-    received = lax.all_to_all(packed, "exp", split_axis=0, concat_axis=0, tiled=True)
-    gate_pre = jnp.einsum("sucd,udf->sucf", received, gate_full, preferred_element_type=jnp.float32)
-    up_pre = jnp.einsum("sucd,udf->sucf", received, up_full, preferred_element_type=jnp.float32)
-    inner_act = (gate_pre * jax.nn.sigmoid(gate_pre) * up_pre).astype(jnp.bfloat16)
-    result = jnp.einsum(
-        "sucf,ufd->sucd", inner_act, down_full, preferred_element_type=jnp.float32
-    ).astype(jnp.bfloat16)
-    returned = lax.all_to_all(result, "exp", split_axis=0, concat_axis=0, tiled=True)
-    returned, received, gate_pre, up_pre = (returned, received, gate_pre, up_pre)
-    slot_results = returned.reshape(slot_total, width)
-    picked = slot_results[slot_index].reshape(tok_rows, top_count, width)
-    mixture = jnp.sum(gate_shares[:, :, None] * picked.astype(jnp.float32), axis=1)
-    output = (hidden + mixture).astype(jnp.bfloat16)
-    share_grad = jnp.einsum("td,tkd->tk", out_grad, picked, preferred_element_type=jnp.float32)
-    result_grad = (
-        (gate_shares[:, :, None] * out_grad.astype(jnp.float32)[:, None, :])
-        .astype(jnp.bfloat16)
-        .reshape(route_count, width)
-    )
-    packed_grad = jnp.where(filled[:, None] > 0, result_grad[route_of_slot], empty_row)
-    packed_grad = packed_grad.reshape(owner_count, local_experts, capacity, width)
-    arrived = lax.all_to_all(packed_grad, "exp", split_axis=0, concat_axis=0, tiled=True)
+    gates = dense_gates(logits, routes, expert_ids)
+    x_all = lax.all_gather(normed_ffn, "exp", axis=0, tiled=True).reshape(
+        owner_count, tok_rows, width
+    )
+    logits_all = jnp.einsum("std,de->ste", x_all, w_router, preferred_element_type=jnp.float32)
+    gates_all = dense_gates(
+        logits_all.reshape(-1, expert_count), routes_all, expert_ids
+    ).reshape(owner_count, tok_rows, owner_count, local_experts)
+    own_gates = lax.dynamic_index_in_dim(gates_all, exp_index, 2, keepdims=False)
+    slot_gates = jnp.einsum(
+        "usct,stu->usc", dispatch, own_gates, precision=lax.Precision.HIGHEST,
+        preferred_element_type=jnp.float32,
+    )
+    received = jnp.einsum(
+        "usct,std->uscd", dispatch, x_all, preferred_element_type=jnp.float32
+    ).astype(jnp.bfloat16).reshape(local_experts, -1, width)
+    slot_gates = slot_gates.reshape(local_experts, -1)
+    gate_pre = jnp.einsum("umd,udf->umf", received, gate_full, preferred_element_type=jnp.float32)
+    up_pre = jnp.einsum("umd,udf->umf", received, up_full, preferred_element_type=jnp.float32)
     sigmoid_gate = jax.nn.sigmoid(gate_pre)
     inner_act = (gate_pre * sigmoid_gate * up_pre).astype(jnp.bfloat16)
-    inner_grad = jnp.einsum(
-        "sucd,ufd->sucf", arrived, down_full, preferred_element_type=jnp.float32
-    )
-    down_part = jnp.einsum("sucf,sucd->ufd", inner_act, arrived, preferred_element_type=jnp.float32)
+    result = jnp.einsum(
+        "umf,ufd->umd", inner_act, down_full, preferred_element_type=jnp.float32
+    ).astype(jnp.bfloat16).astype(jnp.float32)
+    weighted = (slot_gates[..., None] * result).astype(jnp.bfloat16)
+    mixture_part = jnp.einsum(
+        "usct,uscd->std",
+        dispatch,
+        weighted.reshape(local_experts, owner_count, capacity, width),
+        preferred_element_type=jnp.float32,
+    ).astype(jnp.bfloat16)
+    mixture = lax.psum_scatter(
+        mixture_part.reshape(-1, width), "exp", scatter_dimension=0, tiled=True
+    ).astype(jnp.float32)
+    output = (hidden + mixture).astype(jnp.bfloat16)
+    share_slots = jnp.sum(result * og_packed.astype(jnp.float32), axis=2)
+    share_back = jnp.einsum(
+        "usct,usc->sut", dispatch, share_slots.reshape(local_experts, owner_count, capacity),
+        precision=lax.Precision.HIGHEST, preferred_element_type=jnp.float32,
+    )
+    share_grad = (
+        lax.all_to_all(share_back, "exp", split_axis=0, concat_axis=0, tiled=True)
+        .reshape(expert_count, tok_rows)
+        .T
+    )
+    arrived = (slot_gates[..., None] * og_packed.astype(jnp.float32)).astype(jnp.bfloat16)
+    inner_grad = jnp.einsum("umd,ufd->umf", arrived, down_full, preferred_element_type=jnp.float32)
     gate_grad = (
         inner_grad * up_pre * sigmoid_gate * (1.0 + gate_pre * (1.0 - sigmoid_gate))
     ).astype(jnp.bfloat16)
     up_grad = (inner_grad * gate_pre * sigmoid_gate).astype(jnp.bfloat16)
     back_rows = (
-        jnp.einsum("sucf,udf->sucd", gate_grad, gate_full, preferred_element_type=jnp.float32)
-        + jnp.einsum("sucf,udf->sucd", up_grad, up_full, preferred_element_type=jnp.float32)
-    ).astype(jnp.bfloat16)
-    gate_part = jnp.einsum(
-        "sucd,sucf->udf", received, gate_grad, preferred_element_type=jnp.float32
-    )
-    up_part = jnp.einsum("sucd,sucf->udf", received, up_grad, preferred_element_type=jnp.float32)
-    slot_grads = lax.all_to_all(back_rows, "exp", split_axis=0, concat_axis=0, tiled=True).reshape(
-        slot_total, width
-    )
-    ffn_grad = jnp.sum(
-        slot_grads[slot_index].reshape(tok_rows, top_count, width).astype(jnp.float32), axis=1
-    )
-    mixed_grad = gate_shares * (
-        share_grad - jnp.sum(gate_shares * share_grad, axis=1, keepdims=True)
-    )
-    logit_grad = jnp.sum(jnp.where(route_hits, mixed_grad[:, :, None], 0.0), axis=1).astype(
-        jnp.bfloat16
-    )
+        jnp.einsum("umf,udf->umd", gate_grad, gate_full, preferred_element_type=jnp.float32)
+        + jnp.einsum("umf,udf->umd", up_grad, up_full, preferred_element_type=jnp.float32)
+    ).astype(jnp.bfloat16)
+    grad_part = jnp.einsum(
+        "usct,uscd->std",
+        dispatch,
+        back_rows.reshape(local_experts, owner_count, capacity, width),
+        preferred_element_type=jnp.float32,
+    ).astype(jnp.bfloat16)
+    ffn_grad = lax.psum_scatter(
+        grad_part.reshape(-1, width), "exp", scatter_dimension=0, tiled=True
+    ).astype(jnp.float32)
+    down_part = jnp.einsum("umf,umd->ufd", inner_act, arrived, preferred_element_type=jnp.float32)
+    gate_part = jnp.einsum("umd,umf->udf", received, gate_grad, preferred_element_type=jnp.float32)
+    up_part = jnp.einsum("umd,umf->udf", received, up_grad, preferred_element_type=jnp.float32)
+    logit_grad = (
+        gates * (share_grad - jnp.sum(gates * share_grad, axis=1, keepdims=True))
+    ).astype(jnp.bfloat16)
     router_part = contract(normed_ffn, logit_grad, 0, 0)
     ffn_grad = ffn_grad + contract(logit_grad, w_router, 1, 1)
     ffn_part = jnp.sum(ffn_grad * unit_two, axis=0)
@@ -256,9 +285,9 @@
     grads_heads = update
     grads_heads, out_rows = (grads_heads, contract(head_rows, part_rows, 0, 0))
     head_grad = grads_heads.astype(jnp.bfloat16)
-    out_part = lax.dynamic_update_slice_in_dim(
-        jnp.zeros(w_out.shape, jnp.float32), out_rows, tp_index * query_cols, 0
-    )
+    out_weight_grad = lax.all_gather(
+        lax.psum(out_rows.astype(jnp.bfloat16), "exp"), "tp", axis=0, tiled=True
+    ).astype(jnp.float32)
     query_grad, key_grad, value_grad = lax.map(
         attend_backward,
         (
@@ -313,8 +342,8 @@
             jnp.float32
         ),
     )
-    attn_gain_grad, ffn_gain_grad, router_grad, out_weight_grad = lax.psum(
-        (attn_part, ffn_part, router_part, out_part), ("exp", "tp")
+    attn_gain_grad, ffn_gain_grad, router_grad = lax.psum(
+        (attn_part, ffn_part, router_part), ("exp", "tp")
     )
     return (
         output,

time: 1460 us -> 943 us (0.65)
  waiting for transfers between devices: 776 us -> 563 us
  blocking collectives: 259 us -> 63.2 us
  local copies, waits for them, and re-layouts: 134 us -> 38.7 us
  starting transfers between devices: 61.5 us -> 6.79 us
  matrix products: 141 us -> 185 us
    all_to_all x3 -> x1, waiting for transfers between devices: 414 us -> 5.92 us  [shards(): lax.all_to_all(share_back, 'exp', split_axis=0, concat_axis=0, tiled=True)]
    all_to_all x1 -> x0, blocking collectives: 219 us -> none  [shards(): lax.all_to_all(packed_grad, 'exp', split_axis=0, concat_axis=0, tiled=True)]
    reduce_scatter x0 -> x2, waiting for transfers between devices: none -> 175 us  [the longest x1 108 us: shards(): lax.psum_scatter(mixture_part.reshape(-1, width), 'exp', scatter_dimensio...]
    all_gather x0 -> x3, waiting for transfers between devices: none -> 80.1 us  [the longest x1 62.6 us: shards(): lax.all_gather(normed_ffn, 'exp', axis=0, tiled=True)]
    gather x4 -> x0, local copies, waits for them, and re-layouts: 72.6 us -> none  [the longest x1 23.5 us: shards(): result_grad[route_of_slot]]
    all_to_all x3 -> x1, starting transfers between devices: 59.8 us -> 5.55 us  [shards(): lax.all_to_all(share_back, 'exp', split_axis=0, concat_axis=0, tiled=True)]
    dot_general x10 -> x17, matrix products: 112 us -> 152 us  [the longest x1 16.8 us: shards(): jnp.einsum('umd,ufd->umf', arrived, down_full, preferred_element_type=jnp...]
    psum x1, waiting for transfers between devices: 99.7 us -> 60.4 us  [shards(): lax.psum(proj_part[:, :query_cols].astype(jnp.bfloat16), 'exp')]
  transfers between devices with their start and end apart: 15 -> 18, of which waited for: 13 -> 14; matrix products, arithmetic and copies ran while one was open for 10% -> 19% of each run, Pallas kernels for 0% -> 0%
where the time goes in v1:
time: 943 us; the launch traced here: 934 us
  waiting for transfers between devices  563 us (60%)
  matrix products  185 us (20%)
  blocking collectives  63.2 us (7%)
  other arithmetic  61.6 us (7%)
  local copies, waits for them, and re-layouts  38.7 us (4%)
  between operations  16.9 us (2%)
    psum x1, waiting for transfers between devices, shards(): lax.psum((attn_part, ffn_part, router_part), ('exp', 'tp'))  116 us
    reduce_scatter x1, waiting for transfers between devices, shards(): lax.psum_scatter(mixture_part.reshape(-1, width), 'exp', scatter_dimensio...  108 us
    reduce_scatter x1, waiting for transfers between devices, shards(): lax.psum_scatter(grad_part.reshape(-1, width), 'exp', scatter_dimension=0...  67 us
    all_gather x1, waiting for transfers between devices, shards(): lax.all_gather(normed_ffn, 'exp', axis=0, tiled=True)  62.6 us
    psum x1, waiting for transfers between devices, shards(): lax.psum(proj_part[:, :query_cols].astype(jnp.bfloat16), 'exp')  60.4 us
    psum x1, blocking collectives, shards(): lax.psum((attn_part, ffn_part, router_part), ('exp', 'tp'))  40.5 us
    reduce_scatter x1, waiting for transfers between devices, shards(): lax.psum_scatter(jnp.dot(part_rows, out_local, preferred_element_type=jnp...  31.3 us
    all_gather x1, waiting for transfers between devices, shards(): lax.all_gather(w_up, 'tp', axis=2, tiled=True)  22.8 us
  transfers between devices with their start and end apart: 18, of which 14 were waited for; matrix products, arithmetic and copies ran while one was open for 19% of the time, Pallas kernels for 0%

profile of v1, /device:TPU:0, one launch (start us, length us, event | category | flops | bytes accessed | tf_op | source)
XLA Modules:
  0.0 934.5 jit_solution(1334416880597368355)
XLA Ops:
  24.3 11.9 %all-gather.9.cloned.1.call-done = bf16[512,1024]{1,0:T(8,128)(2,1)} async-done(((bf16[256,1024]{1,0:T(8,128)(2,1)}), bf16[512,1024]{1,0:T(8,128)(2,1)}) %all-gather.9.cloned.1.call-update) | async-done | bytes 1048592 | tf_op jit(solution)/shard_map/all_gather | solution.py:170
  61.8 31.3 %reduce-scatter.8.cloned.1.call-done = f32[256,1024]{1,0:T(8,128)} async-done(((f32[512,1024]{1,0:T(8,128)}), f32[256,1024]{1,0:T(8,128)}) %reduce-scatter.8.cloned.1.call-update) | async-done | bytes 1048592 | tf_op jit(solution)/shard_map/reduce_scatter | solution.py:193
  97.9 22.7 %all_gather.28 = s32[4096,8]{0,1:T(8,128)S(1)} all-gather(s32[256,8]{0,1:T(8,128)S(1)} %copy-done.24), channel_id=1, replica_groups=mesh['exp'=16,'tp'=2] {'exp'}, dimensions={0}, use_global_device_ids=true | all-gather | bytes 139264 | tf_op jit(solution)/shard_map/all_gather | solution.py:143
  122.2 17.5 %all-gather.19.cloned.1.call-done = bf16[4096,1024]{1,0:T(8,128)(2,1)} async-done(((bf16[256,1024]{1,0:T(8,128)(2,1)}), bf16[4096,1024]{1,0:T(8,128)(2,1)}) %all-gather.19.cloned.1.call-update) | async-done | bytes 8388624 | tf_op jit(solution)/shard_map/all_gather | solution.py:144
  152.8 62.6 %all-gather.11.cloned.1.call-done = bf16[4096,1024]{1,0:T(8,128)(2,1)} async-done(((bf16[256,1024]{1,0:T(8,128)(2,1)}), bf16[4096,1024]{1,0:T(8,128)(2,1)}) %all-gather.11.cloned.1.call-update) | async-done | bytes 8388624 | tf_op jit(solution)/shard_map/all_gather | solution.py:206
  248.3 11.7 %fusion.82 = f32[2,2048,512]{2,1,0:T(8,128)} fusion(bf16[2,2048,1024]{2,1,0:T(8,128)(2,1)} %bitcast.198, bf16[2,1024,512]{2,1,0:T(8,128)(2,1)} %all-gather.13.cloned.1.call-done), kind=kOutput, calls=%fused_computation.164 | convolution fusion | flops 4294967296 | bytes 18874368 | tf_op jit(solution)/shard_map/umd,udf->umf/dot_general | solution.py:222
  260.0 22.8 %all-gather.15.cloned.1.call-done = bf16[2,1024,512]{2,1,0:T(8,128)(2,1)} async-done(((bf16[2,1024,256]{2,1,0:T(8,128)(2,1)}), bf16[2,1024,512]{2,1,0:T(8,128)(2,1)}) %all-gather.15.cloned.1.call-update) | async-done | bytes 2097168 | tf_op jit(solution)/shard_map/all_gather | solution.py:139
  282.9 11.8 %fusion.83 = f32[2,2048,512]{2,1,0:T(8,128)} fusion(bf16[2,2048,1024]{2,1,0:T(8,128)(2,1)} %bitcast.199, bf16[2,1024,512]{2,1,0:T(8,128)(2,1)} %all-gather.15.cloned.1.call-done), kind=kOutput, calls=%fused_computation.165 | convolution fusion | flops 4294967296 | bytes 18874368 | tf_op jit(solution)/shard_map/umd,udf->umf/dot_general | solution.py:223
  294.7 9.1 fusion.2
  303.8 13.7 %all-gather.17.cloned.1.call-done = bf16[2,512,1024]{2,1,0:T(8,128)(2,1)} async-done(((bf16[2,256,1024]{2,1,0:T(8,128)(2,1)}), bf16[2,512,1024]{2,1,0:T(8,128)(2,1)}) %all-gather.17.cloned.1.call-update) | async-done | bytes 2097168 | tf_op jit(solution)/shard_map/all_gather | solution.py:140
  317.5 16.8 %multiply_convert_fusion = (bf16[2,2048,512]{2,1,0:T(8,128)(2,1)}, bf16[2,2048,512]{2,1,0:T(8,128)(2,1)}, bf16[2,2048,512]{2,1,0:T(8,128)(2,1)}) fusion(f32[2,2048,512]{2,1,0:T(8,128)} %fusion.82, f32[2,2048,512]{2,1,0:T(8,128)} %fusion.83, bf16[2,2048,1024]{2,1,0:T(8,128)(2,1)} %fusion.2, bf16[2,512,1024]{2,1,0:T(8,128)(2,1)} %all-gather.17.cloned.1.call-done), kind=kOutput, calls=%fused_computation.19 | convolution fusion | flops 4328521728 | bytes 39845888 | tf_op jit(solution)/shard_map/umd,ufd->umf/dot_general | solution.py:251
  334.3 10.4 %fusion.84 = f32[2,2048,1024]{2,1,0:T(8,128)} fusion(bf16[2,2048,512]{2,1,0:T(8,128)(2,1)} %get-tuple-element.76, bf16[2,1024,512]{2,1,0:T(8,128)(2,1)S(1)} %copy-done.31), kind=kOutput, calls=%fused_computation.166 | convolution fusion | flops 4294967296 | bytes 23068672 | tf_op jit(solution)/shard_map/umf,udf->umd/dot_general | solution.py:257
  344.7 15.4 %add_convert_fusion = bf16[2,2048,1024]{2,1,0:T(8,128)(2,1)} fusion(f32[2,2048,1024]{2,1,0:T(8,128)} %fusion.84, bf16[2,2048,512]{2,1,0:T(8,128)(2,1)} %get-tuple-element.75, bf16[2,1024,512]{2,1,0:T(8,128)(2,1)} %all-gather.15.cloned.1.call-done), kind=kOutput, calls=%fused_computation.9 | convolution fusion | flops 4303355904 | bytes 31457280 | tf_op jit(solution)/shard_map/umf,udf->umd/dot_general | solution.py:258
  369.5 14.9 %fusion.1 = (f32[2,2048]{1,0:T(2,128)S(1)}, bf16[2,2048,1024]{2,1,0:T(8,128)(2,1)}) fusion(f32[2,16,128,1024]{3,2,1,0:T(8,128)} %copy.82, f32[2,2048]{1,0:T(2,128)S(1)} %bitcast.223, bf16[2,2048,512]{2,1,0:T(8,128)(2,1)} %get-tuple-element.77, bf16[2,512,1024]{2,1,0:T(8,128)(2,1)} %all-gather.17.cloned.1.call-done), kind=kOutput, calls=%fused_computation.3 | convolution fusion | flops 4320129024 | bytes 31490048 | tf_op jit(solution)/shard_map/umf,ufd->umd/dot_general | solution.py:226
  403.2 67.0 %reduce-scatter.12.cloned.1.call-done = bf16[256,1024]{1,0:T(8,128)(2,1)} async-done(((bf16[4096,1024]{1,0:T(8,128)(2,1)}), bf16[256,1024]{1,0:T(8,128)(2,1)}) %reduce-scatter.12.cloned.1.call-update) | async-done | bytes 524304 | tf_op jit(solution)/shard_map/reduce_scatter | solution.py:266
  475.9 20.3 %all-gather.21.cloned.1.call-done = bf16[512,1024]{1,0:T(8,128)(2,1)} async-done(((bf16[256,1024]{1,0:T(8,128)(2,1)}), bf16[512,1024]{1,0:T(8,128)(2,1)}) %all-gather.21.cloned.1.call-update) | async-done | bytes 1048592 | tf_op jit(solution)/shard_map/all_gather | solution.py:283
  516.4 10.5 %convolution_convert_fusion.1 = bf16[2,512,1024]{2,1,0:T(8,128)(2,1)} fusion(bf16[2,2048,512]{2,1,0:T(8,128)(2,1)} %get-tuple-element.77, bf16[2,2048,1024]{2,1,0:T(8,128)(2,1)} %fusion.2), kind=kOutput, calls=%fused_computation.44 | convolution fusion | flops 4296015872 | bytes 14680064 | tf_op jit(solution)/shard_map/umf,umd->ufd/dot_general | solution.py:269
  527.2 10.5 %convolution_convert_fusion.3 = bf16[2,1024,512]{2,1,0:T(8,128)(2,1)} fusion(bf16[2,2048,1024]{2,1,0:T(8,128)(2,1)} %bitcast.200, bf16[2,2048,512]{2,1,0:T(8,128)(2,1)} %get-tuple-element.76), kind=kOutput, calls=%fused_computation.46 | convolution fusion | flops 4296015872 | bytes 14680064 | tf_op jit(solution)/shard_map/umd,umf->udf/dot_general | solution.py:270
  537.9 10.6 %convolution_convert_fusion.2 = bf16[2,1024,512]{2,1,0:T(8,128)(2,1)} fusion(bf16[2,2048,1024]{2,1,0:T(8,128)(2,1)} %bitcast.201, bf16[2,2048,512]{2,1,0:T(8,128)(2,1)} %get-tuple-element.75), kind=kOutput, calls=%fused_computation.45 | convolution fusion | flops 4296015872 | bytes 14680064 | tf_op jit(solution)/shard_map/umd,umf->udf/dot_general | solution.py:271
  559.9 60.4 %all-reduce.7.cloned.1.call-done = (bf16[1024,512]{1,0:T(8,128)(2,1)}, bf16[1024,256]{1,0:T(8,128)(2,1)}, bf16[1024,256]{1,0:T(8,128)(2,1)}, bf16[512,1024]{1,0:T(8,128)(2,1)}) async-done(((bf16[1024,512]{1,0:T(8,128)(2,1)}, bf16[1024,256]{1,0:T(8,128)(2,1)}, bf16[1024,256]{1,0:T(8,128)(2,1)}, bf16[512,1024]{1,0:T(8,128)(2,1)}), (bf16[1024,512]{1,0:T(8,128)(2,1)}, bf16[1024,256]{1,0:T(8,128)(2,1)}, ...) | async-done | bytes 3145744 | tf_op jit(solution)/shard_map/psum | solution.py:337
  637.9 13.4 %reduce-scatter.14.cloned.1.call-done = bf16[256,1024]{1,0:T(8,128)(2,1)} async-done(((bf16[512,1024]{1,0:T(8,128)(2,1)}), bf16[256,1024]{1,0:T(8,128)(2,1)}) %reduce-scatter.14.cloned.1.call-update) | async-done | bytes 524304 | tf_op jit(solution)/shard_map/reduce_scatter | solution.py:314
  653.0 107.7 %reduce-scatter.10.cloned.1.call-done = bf16[256,1024]{1,0:T(8,128)(2,1)} async-done(((bf16[4096,1024]{1,0:T(8,128)(2,1)}), bf16[256,1024]{1,0:T(8,128)(2,1)}) %reduce-scatter.10.cloned.1.call-update) | async-done | bytes 524304 | tf_op jit(solution)/shard_map/reduce_scatter | solution.py:236
  764.2 40.5 %all-reduce = (f32[1024]{0:T(1024)}, f32[1024]{0:T(1024)}) all-reduce(f32[1024]{0:T(1024)S(1)} %get-tuple-element.55, f32[1024]{0:T(1024)S(1)} %get-tuple-element.53), channel_id=1, replica_groups=mesh['exp'=16,'tp'=2] {'exp','tp'}, use_global_device_ids=true, to_apply=%region_23.24 | all-reduce | flops 2048 | bytes 16384 | tf_op jit(solution)/shard_map/psum | solution.py:345
  808.8 116.2 %all-reduce.5.cloned.1.call-done = f32[1024,32]{0,1:T(8,128)} async-done(((f32[1024,32]{0,1:T(8,128)}), f32[1024,32]{0,1:T(8,128)}) %all-reduce.5.cloned.1.call-update) | async-done | bytes 131088 | tf_op jit(solution)/shard_map/psum | solution.py:345
  (210 shorter events, 187.7 us)
Async XLA Ops:
  8.0 51.1 %copy-start = (bf16[1024,1024]{1,0:T(8,128)(2,1)S(1)}, bf16[1024,1024]{1,0:T(8,128)(2,1)}, u32[]{:S(2)}) copy-start(bf16[1024,1024]{1,0:T(8,128)(2,1)} %param.19) | copy-start | bytes 6291460
  8.0 28.2 %all-gather.9.cloned.1.call-start = ((), (), s32[]{:S(2)}) async-start(), calls=%async_computation.8 | async-start | bytes 1572864 | tf_op jit(solution)/shard_map/all_gather | solution.py:170
  12.0 81.1 %reduce-scatter.8.cloned.1.call-start = ((), (), s32[]{:S(2)}) async-start(), calls=%async_computation.9 | async-start | bytes 3145728 | tf_op jit(solution)/shard_map/reduce_scatter | solution.py:193
  58.3 36.5 %copy-start.20 = (f32[1024]{0:T(1024)S(1)}, f32[1024]{0:T(1024)}, u32[]{:S(2)}) copy-start(f32[1024]{0:T(1024)} %param.20) | copy-start | bytes 12292
  58.3 39.6 %copy-start.24 = (s32[256,8]{0,1:T(8,128)S(1)}, s32[256,8]{0,1:T(8,128)}, u32[]{:S(2)}) copy-start(s32[256,8]{0,1:T(8,128)} %param.26) | copy-start | bytes 24580
  61.2 78.6 %all-gather.19.cloned.1.call-start = ((), (), s32[]{:S(2)}) async-start(), calls=%async_computation.15 | async-start | bytes 8912896 | tf_op jit(solution)/shard_map/all_gather | solution.py:144
  61.7 153.7 %all-gather.11.cloned.1.call-start = ((), (), s32[]{:S(2)}) async-start(), calls=%async_computation.10 | async-start | bytes 8912896 | tf_op jit(solution)/shard_map/all_gather | solution.py:206
  95.7 152.6 %all-gather.13.cloned.1.call-start = ((), (), s32[]{:S(2)}) async-start(), calls=%async_computation.11 | async-start | bytes 3145728 | tf_op jit(solution)/shard_map/all_gather | solution.py:138
  96.3 186.6 %all-gather.15.cloned.1.call-start = ((), (), s32[]{:S(2)}) async-start(), calls=%async_computation.12 | async-start | bytes 3145728 | tf_op jit(solution)/shard_map/all_gather | solution.py:139
  97.0 220.5 %all-gather.17.cloned.1.call-start = ((), (), s32[]{:S(2)}) async-start(), calls=%async_computation.13 | async-start | bytes 3145728 | tf_op jit(solution)/shard_map/all_gather | solution.py:140
  97.8 372.4 %reduce-scatter.12.cloned.1.call-start = ((), (), s32[]{:S(2)}) async-start(), calls=%async_computation.16 | async-start | bytes 8912896 | tf_op jit(solution)/shard_map/reduce_scatter | solution.py:266
  146.7 68.7 %copy-start.13 = (bf16[1024,32]{0,1:T(8,128)(2,1)S(1)}, bf16[1024,32]{0,1:T(8,128)(2,1)}, u32[]{:S(2)}) copy-start(bf16[1024,32]{0,1:T(8,128)(2,1)} %param.21) | copy-start | bytes 196612
  387.9 12.2 %all-to-all-start = ((f32[16,2,256]{2,1,0:T(2,128)}), f32[16,2,256]{2,1,0:T(2,128)}, u32[]{:S(2)}, u32[]{:S(2)}) async-start(f32[16,2,256]{2,1,0:T(2,128)} %bitcast.225), calls=%async_computation.3 | async-start | bytes 65536 | tf_op jit(solution)/shard_map/all_to_all | solution.py:246
  393.5 102.7 %all-gather.21.cloned.1.call-start = ((), (), s32[]{:S(2)}) async-start(), calls=%async_computation.17 | async-start | bytes 1572864 | tf_op jit(solution)/shard_map/all_gather | solution.py:283
  475.1 145.2 %all-reduce.7.cloned.1.call-start = ((), (), s32[]{:S(2)}) async-start(), calls=%async_computation.24 | async-start | bytes 6291456 | tf_op jit(solution)/shard_map/psum | solution.py:337
  516.4 106.3 %reduce-scatter.20.cloned.1.call-start = ((), (), s32[]{:S(2)}) async-start(), calls=%async_computation.23 | async-start | bytes 3145728 | tf_op jit(solution)/shard_map/reduce_scatter | solution.py:332
  526.9 98.5 %reduce-scatter.16.cloned.1.call-start = ((), (), s32[]{:S(2)}) async-start(), calls=%async_computation.21 | async-start | bytes 3145728 | tf_op jit(solution)/shard_map/reduce_scatter | solution.py:326
  537.8 90.4 %reduce-scatter.18.cloned.1.call-start = ((), (), s32[]{:S(2)}) async-start(), calls=%async_computation.22 | async-start | bytes 3145728 | tf_op jit(solution)/shard_map/reduce_scatter | solution.py:329
  548.5 102.8 %reduce-scatter.14.cloned.1.call-start = ((), (), s32[]{:S(2)}) async-start(), calls=%async_computation.18 | async-start | bytes 1572864 | tf_op jit(solution)/shard_map/reduce_scatter | solution.py:314
  552.7 208.0 %reduce-scatter.10.cloned.1.call-start = ((), (), s32[]{:S(2)}) async-start(), calls=%async_computation.14 | async-start | bytes 8912896 | tf_op jit(solution)/shard_map/reduce_scatter | solution.py:236
  559.9 244.9 %all-gather.23.cloned.1.call-start = ((), (), s32[]{:S(2)}) async-start(), calls=%async_computation.19 | async-start | bytes 3145728 | tf_op jit(solution)/shard_map/all_gather | solution.py:288
  620.4 304.6 %all-reduce.5.cloned.1.call-start = ((), (), s32[]{:S(2)}) async-start(), calls=%async_computation.20 | async-start | bytes 262144 | tf_op jit(solution)/shard_map/psum | solution.py:345
  622.6 138.1 %copy-start.21 = (f32[1024]{0:T(1024)S(1)}, f32[1024]{0:T(1024)}, u32[]{:S(2)}) copy-start(f32[1024]{0:T(1024)} %param.20) | copy-start | bytes 12292
  622.6 138.1 %copy-start.27 = (f32[256]{0:T(256)S(1)}, f32[256]{0:T(256)}, u32[]{:S(2)}) copy-start(f32[256]{0:T(256)} %copy-done.26) | copy-start | bytes 3076
  (30 other events, 205.2 us)
Sparse Core Ops, SparseCore 0:
  12.2 23.9 all-gather.8
  61.3 31.8 reduce-scatter.7
  475.2 20.9 all-gather.20
  527.1 31.8 reduce-scatter.19
  561.6 31.8 reduce-scatter.15
  596.2 31.8 reduce-scatter.17
  631.0 20.3 reduce-scatter.13
  655.9 104.7 reduce-scatter.9
  762.3 33.3 all-gather.22
  802.5 122.3 all-reduce.4
Sparse Core Ops, SparseCore 1:
  64.0 75.6 all-gather.18
  142.6 72.8 all-gather.10
  216.9 31.3 all-gather.12
  249.9 32.9 all-gather.14
  284.5 32.9 all-gather.16
  366.9 103.2 reduce-scatter.11
  516.4 103.8 all-reduce.6

commit v2 on v1

--- a/solution.py
+++ b/solution.py
@@ -96,6 +96,48 @@
         preferred_element_type=jnp.float32,
     )
     return (query_grad.reshape(queries.shape[0], -1), key_grad, value_grad)
+
+
+def tp_blocks(block):
+    count = lax.axis_size("tp")
+    return [block] + [
+        lax.ppermute(block, "tp", [(j, (j - k) % count) for j in range(count)])
+        for k in range(1, count)
+    ]
+
+
+def tp_sum(parts):
+    count = lax.axis_size("tp")
+    total = parts[0].astype(jnp.float32)
+    for k in range(1, count):
+        moved = lax.ppermute(parts[k], "tp", [(j, (j + k) % count) for j in range(count)])
+        total = total + moved.astype(jnp.float32)
+    return total
+
+
+def tp_gather_rows(block):
+    count, rows = lax.axis_size("tp"), block.shape[0]
+    whole = jnp.zeros((count * rows, block.shape[1]), block.dtype)
+    for k, piece in enumerate(tp_blocks(block)):
+        start = lax.rem(lax.axis_index("tp") + k, count) * rows
+        whole = lax.dynamic_update_slice_in_dim(whole, piece, start, 0)
+    return whole
+
+
+def tp_scatter_rows(whole, rows):
+    count = lax.axis_size("tp")
+    return tp_sum(
+        [
+            lax.dynamic_slice_in_dim(
+                whole, lax.rem(lax.axis_index("tp") + k, count) * rows, rows, 0
+            )
+            for k in range(count)
+        ]
+    )
+
+
+def tp_scatter_units(whole, axis):
+    return tp_sum(jnp.split(whole.astype(jnp.bfloat16), lax.axis_size("tp"), axis=axis))
 
 
 def dense_gates(logits, routes, expert_ids):
@@ -135,12 +177,16 @@
     local_experts = w_gate.shape[0]
     owner_count = lax.axis_size("exp")
     gate_full, up_full, down_full = (
-        lax.all_gather(w_gate, "tp", axis=2, tiled=True),
-        lax.all_gather(w_up, "tp", axis=2, tiled=True),
-        lax.all_gather(w_down, "tp", axis=1, tiled=True),
+        jnp.concatenate(tp_blocks(w_gate), axis=2),
+        jnp.concatenate(tp_blocks(w_up), axis=2),
+        jnp.concatenate(tp_blocks(w_down), axis=1),
     )
     exp_index = lax.axis_index("exp")
-    routes_all = lax.all_gather(routes, "exp", axis=0, tiled=True)
+    routes_all = (
+        lax.all_gather(routes.T.astype(jnp.float32), "exp", axis=1, tiled=True)
+        .astype(jnp.int32)
+        .T
+    )
     og_all = lax.all_gather(out_grad, "exp", axis=0, tiled=True)
     own_ids = exp_index * local_experts + jnp.arange(local_experts, dtype=jnp.int32)
     own_hits = jnp.any(
@@ -167,7 +213,7 @@
     scale_one = lax.rsqrt(jnp.mean(source * source, axis=1, keepdims=True) + epsilon)
     unit_one = source * scale_one
     normed = (unit_one * gain_attn).astype(jnp.bfloat16)
-    gathered = lax.all_gather(normed, "tp", axis=0, tiled=True)
+    gathered = tp_gather_rows(normed)
     w_proj = jnp.concatenate([w_query, w_key, w_value], axis=1)
     projected = jnp.dot(gathered, w_proj, preferred_element_type=jnp.float32)
     seq_rows = segment_ids.reshape(seq_count, seq_len)
@@ -190,11 +236,8 @@
     head_rows = attended.reshape(group_rows, query_cols).astype(jnp.bfloat16)
     out_local = lax.dynamic_slice_in_dim(w_out, tp_index * query_cols, query_cols, 0)
     part_rows = head_rows
-    branch = lax.psum_scatter(
-        jnp.dot(part_rows, out_local, preferred_element_type=jnp.float32),
-        "tp",
-        scatter_dimension=0,
-        tiled=True,
+    branch = tp_scatter_rows(
+        jnp.dot(part_rows, out_local, preferred_element_type=jnp.float32), tok_rows
     )
     hidden = source + branch
     scale_two = lax.rsqrt(jnp.mean(hidden * hidden, axis=1, keepdims=True) + epsilon)
@@ -203,7 +246,10 @@
     logits = jnp.dot(normed_ffn, w_router, preferred_element_type=jnp.float32)
     expert_ids = jnp.arange(expert_count, dtype=jnp.int32)
     gates = dense_gates(logits, routes, expert_ids)
-    x_all = lax.all_gather(normed_ffn, "exp", axis=0, tiled=True).reshape(
+    x_send, gate_full, up_full, down_full = lax.optimization_barrier(
+        (normed_ffn, gate_full, up_full, down_full)
+    )
+    x_all = lax.all_gather(x_send, "exp", axis=0, tiled=True).reshape(
         owner_count, tok_rows, width
     )
     logits_all = jnp.einsum("std,de->ste", x_all, w_router, preferred_element_type=jnp.float32)
@@ -233,6 +279,7 @@
         weighted.reshape(local_experts, owner_count, capacity, width),
         preferred_element_type=jnp.float32,
     ).astype(jnp.bfloat16)
+    og_packed, mixture_part = lax.optimization_barrier((og_packed, mixture_part))
     mixture = lax.psum_scatter(
         mixture_part.reshape(-1, width), "exp", scatter_dimension=0, tiled=True
     ).astype(jnp.float32)
@@ -280,13 +327,18 @@
         unit_grad_two - unit_two * jnp.mean(unit_grad_two * unit_two, axis=1, keepdims=True)
     )
     branch_low = hidden_grad.astype(jnp.bfloat16)
-    part_rows = lax.all_gather(branch_low, "tp", axis=0, tiled=True)
+    part_rows = tp_gather_rows(branch_low)
     update = contract(part_rows, out_local, 1, 1)
     grads_heads = update
     grads_heads, out_rows = (grads_heads, contract(head_rows, part_rows, 0, 0))
     head_grad = grads_heads.astype(jnp.bfloat16)
     out_weight_grad = lax.all_gather(
-        lax.psum(out_rows.astype(jnp.bfloat16), "exp"), "tp", axis=0, tiled=True
+        lax.psum_scatter(
+            out_rows.astype(jnp.bfloat16), "exp", scatter_dimension=0, tiled=True
+        ),
+        ("tp", "exp"),
+        axis=0,
+        tiled=True,
     ).astype(jnp.float32)
     query_grad, key_grad, value_grad = lax.map(
         attend_backward,
@@ -311,40 +363,36 @@
     ).astype(jnp.bfloat16)
     proj_part = contract(gathered, proj_grad, 0, 0)
     part_rows = proj_grad
-    normed_grad = lax.psum_scatter(
-        contract(part_rows, w_proj, 1, 1).astype(jnp.bfloat16),
-        "tp",
-        scatter_dimension=0,
-        tiled=True,
-    ).astype(jnp.float32)
+    normed_grad = tp_scatter_rows(
+        contract(part_rows, w_proj, 1, 1).astype(jnp.bfloat16), tok_rows
+    )
     attn_part = jnp.sum(normed_grad * unit_one, axis=0)
     unit_grad_one = normed_grad * gain_attn
     input_grad = hidden_grad + scale_one * (
         unit_grad_one - unit_one * jnp.mean(unit_grad_one * unit_one, axis=1, keepdims=True)
     )
     gate_weight_grad, up_weight_grad, down_weight_grad = (
-        lax.psum_scatter(
-            gate_part.astype(jnp.bfloat16), "tp", scatter_dimension=2, tiled=True
-        ).astype(jnp.float32),
-        lax.psum_scatter(
-            up_part.astype(jnp.bfloat16), "tp", scatter_dimension=2, tiled=True
-        ).astype(jnp.float32),
-        lax.psum_scatter(
-            down_part.astype(jnp.bfloat16), "tp", scatter_dimension=1, tiled=True
-        ).astype(jnp.float32),
-    )
+        tp_scatter_units(gate_part, 2),
+        tp_scatter_units(up_part, 2),
+        tp_scatter_units(down_part, 1),
+    )
+    proj_low, output = lax.optimization_barrier((proj_part.astype(jnp.bfloat16), output))
+    proj_sum = lax.all_gather(
+        lax.psum_scatter(proj_low, "exp", scatter_dimension=0, tiled=True),
+        "exp",
+        axis=0,
+        tiled=True,
+    ).astype(jnp.float32)
     query_weight_grad, key_weight_grad, value_weight_grad = (
-        lax.psum(proj_part[:, :query_cols].astype(jnp.bfloat16), "exp").astype(jnp.float32),
-        lax.psum(
-            proj_part[:, query_cols : query_cols + kv_cols].astype(jnp.bfloat16), "exp"
-        ).astype(jnp.float32),
-        lax.psum(proj_part[:, query_cols + kv_cols :].astype(jnp.bfloat16), "exp").astype(
-            jnp.float32
-        ),
-    )
-    attn_gain_grad, ffn_gain_grad, router_grad = lax.psum(
-        (attn_part, ffn_part, router_part), ("exp", "tp")
-    )
+        proj_sum[:, :query_cols],
+        proj_sum[:, query_cols : query_cols + kv_cols],
+        proj_sum[:, query_cols + kv_cols :],
+    )
+    attn_gain_grad = jnp.sum(
+        lax.all_gather(attn_part[None, :], ("exp", "tp"), axis=0, tiled=True), axis=0
+    )
+    small = lax.psum(jnp.concatenate([router_part, ffn_part[:, None]], axis=1), ("exp", "tp"))
+    router_grad, ffn_gain_grad = small[:, :expert_count], small[:, expert_count]
     return (
         output,
         input_grad,

time: 943 us -> 890 us (0.944)
  waiting for transfers between devices: 563 us -> 464 us
  blocking collectives: 63.2 us -> 89.8 us
  local copies, waits for them, and re-layouts: 38.7 us -> 55.2 us
  starting transfers between devices: 6.79 us -> 18.5 us
  matrix products: 185 us -> 175 us
    psum x2 -> x1, waiting for transfers between devices: 177 us -> 44.2 us  [shards(): lax.psum(jnp.concatenate([router_part, ffn_part[:, None]], axis=1), ('exp...]
    ppermute x0 -> x10, waiting for transfers between devices: none -> 113 us  [the longest x5 63.8 us: tp_sum(): lax.ppermute(parts[k], 'tp', [(j, (j + k) % count) for j in range(count)])]
    all_gather x7 -> x3, waiting for transfers between devices: 140 us -> 60.6 us  [the longest x1 31.5 us: shards(): lax.all_gather(x_send, 'exp', axis=0, tiled=True)]
    reduce_scatter x5 -> x2, waiting for transfers between devices: 44.8 us -> 120 us  [the longest x1 64.9 us: shards(): lax.psum_scatter(proj_low, 'exp', scatter_dimension=0, tiled=True)]
    all_gather x1 -> x2, blocking collectives: 22.7 us -> 89.8 us  [the longest x1 67.2 us: shards(): lax.all_gather(attn_part[None, :], ('exp', 'tp'), axis=0, tiled=True)]
    reduce_scatter x1, waiting for transfers between devices: 108 us -> 44.5 us  [shards(): lax.psum_scatter(mixture_part.reshape(-1, width), 'exp', scatter_dimensio...]
    psum x1 -> x0, blocking collectives: 40.5 us -> none  [shards(): lax.psum((attn_part, ffn_part, router_part), ('exp', 'tp'))]
    convert_element_type x10 -> x2, other arithmetic: 32.6 us -> 4.07 us  [the longest x1 4.07 us: shards(): out_weight_grad = lax.all_gather(lax.psum_scatter(out_rows.astype(jnp.bfl...]
  transfers between devices with their start and end apart: 18 -> 20, of which waited for: 14 -> 17; matrix products, arithmetic and copies ran while one was open for 19% -> 20% of each run, Pallas kernels for 0% -> 0%
where the time goes in v2:
time: 890 us; the launch traced here: 880 us
  waiting for transfers between devices  464 us (52%)
  matrix products  175 us (20%)
  blocking collectives  89.8 us (10%)
  other arithmetic  61.7 us (7%)
  local copies, waits for them, and re-layouts  55.2 us (6%)
  starting transfers between devices  18.5 us (2%)
  between operations  15.1 us (2%)
    reduce_scatter x1, waiting for transfers between devices, shards(): lax.psum_scatter(grad_part.reshape(-1, width), 'exp', scatter_dimension=0...  74.5 us
    all_gather x1, blocking collectives, shards(): lax.all_gather(attn_part[None, :], ('exp', 'tp'), axis=0, tiled=True)  67.2 us
    reduce_scatter x1, waiting for transfers between devices, shards(): lax.psum_scatter(proj_low, 'exp', scatter_dimension=0, tiled=True)  64.9 us
    ppermute x5, waiting for transfers between devices, tp_sum(): lax.ppermute(parts[k], 'tp', [(j, (j + k) % count) for j in range(count)])  63.8 us
    reduce_scatter x1, waiting for transfers between devices, shards(): lax.psum_scatter(out_rows.astype(jnp.bfloat16), 'exp', scatter_dimension=...  55.4 us
    ppermute x5, waiting for transfers between devices, tp_blocks(): lax.ppermute(block, 'tp', [(j, (j - k) % count) for j in range(count)])  49.5 us
    reduce_scatter x1, waiting for transfers between devices, shards(): lax.psum_scatter(mixture_part.reshape(-1, width), 'exp', scatter_dimensio...  44.5 us
    psum x1, waiting for transfers between devices, shards(): lax.psum(jnp.concatenate([router_part, ffn_part[:, None]], axis=1), ('exp...  44.2 us
  transfers between devices with their start and end apart: 20, of which 17 were waited for; matrix products, arithmetic and copies ran while one was open for 20% of the time, Pallas kernels for 0%

profile of v2, /device:TPU:0, one launch (start us, length us, event | category | flops | bytes accessed | tf_op | source)
XLA Modules:
  0.0 880.3 jit_solution(2187262453539777103)
XLA Ops:
  56.8 16.8 %collective-permute-done.3 = bf16[2,1024,256]{2,1,0:T(8,128)(2,1)} collective-permute-done((bf16[2,1024,256]{2,1,0:T(8,128)(2,1)}, bf16[2,1024,256]{2,1,0:T(8,128)(2,1)}, u32[]{:S(2)}, u32[]{:S(2)}) %collective-permute-start.3) | collective-permute-done | bytes 1048608 | tf_op jit(solution)/shard_map/ppermute | solution.py:104
  76.3 19.8 %collective-permute-done.4 = bf16[2,256,1024]{2,1,0:T(8,128)(2,1)} collective-permute-done((bf16[2,256,1024]{2,1,0:T(8,128)(2,1)}, bf16[2,256,1024]{2,1,0:T(8,128)(2,1)}, u32[]{:S(2)}, u32[]{:S(2)}) %collective-permute-start.4) | collective-permute-done | bytes 1048608 | tf_op jit(solution)/shard_map/ppermute | solution.py:104
  98.8 18.8 %collective-permute-done.1 = f32[256,1024]{1,0:T(8,128)S(1)} collective-permute-done((f32[256,1024]{1,0:T(8,128)S(1)}, f32[256,1024]{1,0:T(8,128)S(1)}, u32[]{:S(2)}, u32[]{:S(2)}) %collective-permute-start.1) | collective-permute-done | bytes 1048608 | tf_op jit(solution)/shard_map/ppermute | solution.py:113
  119.0 22.7 %all_gather.18 = f32[8,4096]{1,0:T(8,128)S(1)} all-gather(f32[8,256]{1,0:T(8,128)S(1)} %convert_bitcast_fusion.2), channel_id=1, replica_groups=mesh['exp'=16,'tp'=2] {'exp'}, dimensions={1}, use_global_device_ids=true | all-gather | bytes 139264 | tf_op jit(solution)/shard_map/all_gather | solution.py:186
  145.0 11.0 %convert_bitcast_fusion.1 = bf16[2,16,128,1024]{3,2,0,1:T(8,128)(2,1)} fusion(bf16[16,256,1024,1]{2,1,3,0:T(8,128)(2,1)} %bitcast.196, s32[2,16,256]{2,0,1:T(2,128)S(1)} %copy.97), kind=kOutput, calls=%fused_computation.22 | convolution fusion | flops 2152726528 | bytes 16809984 | tf_op jit(solution)/shard_map/usct,std->uscd/dot_general | solution.py:206
  164.1 31.5 %all-gather.6.cloned.1.call-done = bf16[4096,1024]{1,0:T(8,128)(2,1)} async-done(((bf16[256,1024]{1,0:T(8,128)(2,1)}), bf16[4096,1024]{1,0:T(8,128)(2,1)}) %all-gather.6.cloned.1.call-update) | async-done | bytes 8388624 | tf_op jit(solution)/shard_map/all_gather | solution.py:252
  227.7 11.1 %multiply_convert_fusion.2 = (bf16[2,2048,512]{2,1,0:T(8,128)(2,1)}, f32[2,2048,512]{2,1,0:T(8,128)}) fusion(f32[2,2048,512]{2,1,0:T(8,128)} %fusion.92, bf16[2,2048,1024]{2,1,0:T(8,128)(2,1)S(1)} %bitcast.201, bf16[2,1024,512]{2,1,0:T(8,128)(2,1)} %pad_maximum_fusion.1), kind=kOutput, calls=%fused_computation.19 | convolution fusion | flops 4307550208 | bytes 31457280 | tf_op jit(solution)/shard_map/umd,udf->umf/dot_general | solution.py:269
  238.7 9.3 %fusion = (bf16[2,2048,1024]{2,1,0:T(8,128)(2,1)S(1)}, bf16[2,2048,1024]{2,1,0:T(8,128)(2,1)}) fusion(f32[2,2048]{1,0:T(2,128)S(1)} %bitcast.231, bf16[2,2048,512]{2,1,0:T(8,128)(2,1)} %get-tuple-element.111, bf16[2,512,1024]{2,1,0:T(8,128)(2,1)} %pad_maximum_fusion.2), kind=kOutput, calls=%fused_computation.3 | convolution fusion | flops 4311744512 | bytes 23085056 | tf_op jit(solution)/shard_map/umf,ufd->umd/dot_general | solution.py:272
  253.1 14.6 %multiply_convert_fusion = (bf16[2,2048,512]{2,1,0:T(8,128)(2,1)}, bf16[2,2048,512]{2,1,0:T(8,128)(2,1)}) fusion(f32[2,2048,512]{2,1,0:T(8,128)} %fusion.92, f32[2,2048,512]{2,1,0:T(8,128)} %get-tuple-element.112, bf16[2,512,1024]{2,1,0:T(8,128)(2,1)} %pad_maximum_fusion.2, bf16[2,2048,1024]{2,1,0:T(8,128)(2,1)} %bitcast.191, f32[2,2048]{1,0:T(2,128)S(1)} %bitcast.232), kind=kOutput, calls=%fused_computation.17 | convolution fusion | flops 4334813184 | bytes 35667968 | tf_op jit(solution)/shard_map/umd,ufd->umf/dot_general | solution.py:298
  267.8 10.5 %fusion.93 = f32[2,2048,1024]{2,1,0:T(8,128)} fusion(bf16[2,2048,512]{2,1,0:T(8,128)(2,1)} %get-tuple-element.90, bf16[2,1024,512]{2,1,0:T(8,128)(2,1)S(1)} %copy-done.14), kind=kOutput, calls=%fused_computation.183 | convolution fusion | flops 4294967296 | bytes 23068672 | tf_op jit(solution)/shard_map/umf,udf->umd/dot_general | solution.py:304
  278.2 15.4 %add_convert_fusion = bf16[2,2048,1024]{2,1,0:T(8,128)(2,1)} fusion(f32[2,2048,1024]{2,1,0:T(8,128)} %fusion.93, bf16[2,2048,512]{2,1,0:T(8,128)(2,1)} %get-tuple-element.89, bf16[2,1024,512]{2,1,0:T(8,128)(2,1)} %pad_maximum_fusion.1), kind=kOutput, calls=%fused_computation.8 | convolution fusion | flops 4303355904 | bytes 31457280 | tf_op jit(solution)/shard_map/umf,udf->umd/dot_general | solution.py:305
  303.0 9.5 %fusion.2 = f32[2,2048]{1,0:T(2,128)S(1)} fusion(bf16[2,2048,1024]{2,1,0:T(8,128)(2,1)} %bitcast.192, bf16[2,2048,1024]{2,1,0:T(8,128)(2,1)} %get-tuple-element.116), kind=kLoop, calls=%fused_computation.5 | loop fusion | flops 16773120 | bytes 16793600 | tf_op jit(solution)/shard_map/reduce_sum | solution.py:287
  329.0 74.5 %reduce-scatter.5.cloned.1.call-done = bf16[256,1024]{1,0:T(8,128)(2,1)} async-done(((bf16[4096,1024]{1,0:T(8,128)(2,1)}), bf16[256,1024]{1,0:T(8,128)(2,1)}) %reduce-scatter.5.cloned.1.call-update) | async-done | bytes 524304 | tf_op jit(solution)/shard_map/reduce_scatter | solution.py:313
  409.8 11.5 %collective-permute-done.5 = bf16[256,1024]{1,0:T(8,128)(2,1)S(1)} collective-permute-done((bf16[256,1024]{1,0:T(8,128)(2,1)S(1)}, bf16[256,1024]{1,0:T(8,128)(2,1)S(1)}, u32[]{:S(2)}, u32[]{:S(2)}) %collective-permute-start.5) | collective-permute-done | bytes 524320 | tf_op jit(solution)/shard_map/ppermute | solution.py:104
  467.3 44.5 %reduce-scatter.7.cloned.1.call-done = bf16[256,1024]{1,0:T(8,128)(2,1)} async-done(((bf16[4096,1024]{1,0:T(8,128)(2,1)}), bf16[256,1024]{1,0:T(8,128)(2,1)}) %reduce-scatter.7.cloned.1.call-update) | async-done | bytes 524304 | tf_op jit(solution)/shard_map/reduce_scatter | solution.py:283
  517.5 55.4 %reduce-scatter.11.cloned.1.call-done = bf16[32,1024]{1,0:T(8,128)(2,1)} async-done(((bf16[512,1024]{1,0:T(8,128)(2,1)}), bf16[32,1024]{1,0:T(8,128)(2,1)}) %reduce-scatter.11.cloned.1.call-update) | async-done | bytes 65552 | tf_op jit(solution)/shard_map/reduce_scatter | solution.py:336
  573.3 64.9 %reduce-scatter.9.cloned.1.call-done = bf16[64,1024]{1,0:T(8,128)(2,1)} async-done(((bf16[1024,1024]{1,0:T(8,128)(2,1)}), bf16[64,1024]{1,0:T(8,128)(2,1)}) %reduce-scatter.9.cloned.1.call-update) | async-done | bytes 131088 | tf_op jit(solution)/shard_map/reduce_scatter | solution.py:381
  638.2 9.4 %fusion.27 = bf16[2,512,1024]{2,1,0:T(8,128)(2,1)S(1)} fusion(bf16[2,2048,512]{2,1,0:T(8,128)(2,1)} %get-tuple-element.111, bf16[2,2048,1024]{2,1,0:T(8,128)(2,1)} %bitcast.193, f32[2,2048]{1,0:T(2,128)S(1)} %bitcast.233), kind=kOutput, calls=%fused_computation.52 | convolution fusion | flops 4308598784 | bytes 14696448 | tf_op jit(solution)/shard_map/umf,umd->ufd/dot_general | solution.py:316
  651.4 10.8 %convolution_convert_fusion.1 = bf16[2,1024,512]{2,1,0:T(8,128)(2,1)} fusion(bf16[2,2048,1024]{2,1,0:T(8,128)(2,1)} %bitcast.199, bf16[2,2048,512]{2,1,0:T(8,128)(2,1)} %get-tuple-element.89), kind=kOutput, calls=%fused_computation.53 | convolution fusion | flops 4296015872 | bytes 14680064 | tf_op jit(solution)/shard_map/umd,umf->udf/dot_general | solution.py:318
  679.9 19.6 %collective-permute-done.8 = bf16[2,1024,256]{2,1,0:T(8,128)(2,1)} collective-permute-done((bf16[2,1024,256]{2,1,0:T(8,128)(2,1)}, bf16[2,1024,256]{2,1,0:T(8,128)(2,1)}, u32[]{:S(2)}, u32[]{:S(2)}) %collective-permute-start.8) | collective-permute-done | bytes 1048608 | tf_op jit(solution)/shard_map/ppermute | solution.py:113
  702.2 17.0 %collective-permute-done.7 = bf16[2,1024,256]{2,1,0:T(8,128)(2,1)S(1)} collective-permute-done((bf16[2,1024,256]{2,1,0:T(8,128)(2,1)S(1)}, bf16[2,1024,256]{2,1,0:T(8,128)(2,1)S(1)}, u32[]{:S(2)}, u32[]{:S(2)}) %collective-permute-start.7) | collective-permute-done | bytes 1048608 | tf_op jit(solution)/shard_map/ppermute | solution.py:113
  720.7 44.2 %all-reduce.2.cloned.1.call-done = f32[1024,33]{0,1:T(8,128)} async-done(((f32[1024,33]{0,1:T(8,128)}), f32[1024,33]{0,1:T(8,128)}) %all-reduce.2.cloned.1.call-update) | async-done | bytes 135184 | tf_op jit(solution)/shard_map/psum | solution.py:394
  767.9 67.2 %all-gather = f32[32768]{0:T(1024)S(1)} all-gather(f32[1024]{0:T(1024)S(1)} %get-tuple-element.81), channel_id=2, replica_groups=mesh['exp'=16,'tp'=2] {'exp','tp'}, dimensions={0}, use_global_device_ids=true | all-gather | bytes 135168 | tf_op jit(solution)/shard_map/all_gather | solution.py:392
  839.8 29.1 %all-gather.10.cloned.1.call-done = bf16[1024,1024]{1,0:T(8,128)(2,1)} async-done(((bf16[64,1024]{1,0:T(8,128)(2,1)}), bf16[1024,1024]{1,0:T(8,128)(2,1)}) %all-gather.10.cloned.1.call-update) | async-done | bytes 2097168 | tf_op jit(solution)/shard_map/all_gather | solution.py:380
  (262 shorter events, 226.2 us)
Async XLA Ops:
  7.2 137.8 %all-gather.8.cloned.1.call-start = ((), (), s32[]{:S(2)}) async-start(), calls=%async_computation.6 | async-start | bytes 8912896 | tf_op jit(solution)/shard_map/all_gather | solution.py:190
  7.9 187.7 %all-gather.6.cloned.1.call-start = ((), (), s32[]{:S(2)}) async-start(), calls=%async_computation.5 | async-start | bytes 8912896 | tf_op jit(solution)/shard_map/all_gather | solution.py:252
  12.6 16.0 %collective-permute-start = (bf16[256,1024]{1,0:T(8,128)(2,1)}, bf16[256,1024]{1,0:T(8,128)(2,1)}, u32[]{:S(2)}, u32[]{:S(2)}) collective-permute-start(bf16[256,1024]{1,0:T(8,128)(2,1)} %get-tuple-element.88), channel_id=1, source_target_pairs={{0,1},{1,0},{2,3},{3,2},{4,5},{5,4},{6,7},{7,6},{8,9},{9,8},{10,11... | collective-permute-start | bytes 1572872 | tf_op jit(solution)/shard_map/ppermute | solution.py:104
  15.6 38.5 %collective-permute-start.2 = (bf16[2,1024,256]{2,1,0:T(8,128)(2,1)}, bf16[2,1024,256]{2,1,0:T(8,128)(2,1)}, u32[]{:S(2)}, u32[]{:S(2)}) collective-permute-start(bf16[2,1024,256]{2,1,0:T(8,128)(2,1)} %param.22), channel_id=1, source_target_pairs={{0,1},{1,0},{2,3},{3,2},{4,5},{5,4},{6,7},{7,6},{8,9},{9,8},{10,11... | collective-permute-start | bytes 3145736 | tf_op jit(solution)/shard_map/ppermute | solution.py:104
  15.6 58.0 %collective-permute-start.3 = (bf16[2,1024,256]{2,1,0:T(8,128)(2,1)}, bf16[2,1024,256]{2,1,0:T(8,128)(2,1)}, u32[]{:S(2)}, u32[]{:S(2)}) collective-permute-start(bf16[2,1024,256]{2,1,0:T(8,128)(2,1)} %param.23), channel_id=1, source_target_pairs={{0,1},{1,0},{2,3},{3,2},{4,5},{5,4},{6,7},{7,6},{8,9},{9,8},{10,11... | collective-permute-start | bytes 3145736 | tf_op jit(solution)/shard_map/ppermute | solution.py:104
  17.6 78.4 %collective-permute-start.4 = (bf16[2,256,1024]{2,1,0:T(8,128)(2,1)}, bf16[2,256,1024]{2,1,0:T(8,128)(2,1)}, u32[]{:S(2)}, u32[]{:S(2)}) collective-permute-start(bf16[2,256,1024]{2,1,0:T(8,128)(2,1)} %param.24), channel_id=1, source_target_pairs={{0,1},{1,0},{2,3},{3,2},{4,5},{5,4},{6,7},{7,6},{8,9},{9,8},{10,11... | collective-permute-start | bytes 3145736 | tf_op jit(solution)/shard_map/ppermute | solution.py:104
  52.1 65.5 %collective-permute-start.1 = (f32[256,1024]{1,0:T(8,128)S(1)}, f32[256,1024]{1,0:T(8,128)S(1)}, u32[]{:S(2)}, u32[]{:S(2)}) collective-permute-start(f32[256,1024]{1,0:T(8,128)S(1)} %constant_dynamic-slice_fusion.1), channel_id=1, source_target_pairs={{0,1},{1,0},{2,3},{3,2},{4,5},{5,4},{6,7},{7,6},{8,9},{9,8},{10,11... | collective-permute-start | bytes 3145736 | tf_op jit(solution)/shard_map/ppermute | solution.py:113
  56.8 60.8 %copy-start.2 = (bf16[256,1024]{1,0:T(8,128)(2,1)S(1)}, bf16[256,1024]{1,0:T(8,128)(2,1)}, u32[]{:S(2)}) copy-start(bf16[256,1024]{1,0:T(8,128)(2,1)} %param.14) | copy-start | bytes 1572868
  118.9 284.6 %reduce-scatter.5.cloned.1.call-start = ((), (), s32[]{:S(2)}) async-start(), calls=%async_computation.7 | async-start | bytes 8912896 | tf_op jit(solution)/shard_map/reduce_scatter | solution.py:313
  300.5 211.2 %reduce-scatter.7.cloned.1.call-start = ((), (), s32[]{:S(2)}) async-start(), calls=%async_computation.8 | async-start | bytes 8912896 | tf_op jit(solution)/shard_map/reduce_scatter | solution.py:283
  316.1 10.7 %all-to-all-start = ((f32[16,2,256]{2,1,0:T(2,128)}), f32[16,2,256]{2,1,0:T(2,128)}, u32[]{:S(2)}, u32[]{:S(2)}) async-start(f32[16,2,256]{2,1,0:T(2,128)} %bitcast.180), calls=%async_computation.1 | async-start | bytes 65536 | tf_op jit(solution)/shard_map/all_to_all | solution.py:293
  320.2 252.8 %reduce-scatter.11.cloned.1.call-start = ((), (), s32[]{:S(2)}) async-start(), calls=%async_computation.11 | async-start | bytes 1114112 | tf_op jit(solution)/shard_map/reduce_scatter | solution.py:336
  329.0 80.1 %copy-start.33 = (bf16[256,32]{0,1:T(8,128)(2,1)}, bf16[256,32]{0,1:T(8,128)(2,1)S(1)}, u32[]{:S(2)}) copy-start(bf16[256,32]{0,1:T(8,128)(2,1)S(1)} %fusion.71) | copy-start | bytes 49156
  407.5 13.8 %collective-permute-start.5 = (bf16[256,1024]{1,0:T(8,128)(2,1)S(1)}, bf16[256,1024]{1,0:T(8,128)(2,1)S(1)}, u32[]{:S(2)}, u32[]{:S(2)}) collective-permute-start(bf16[256,1024]{1,0:T(8,128)(2,1)S(1)} %get-tuple-element.84), channel_id=1, source_target_pairs={{0,1},{1,0},{2,3},{3,2},{4,5},{5,4},{6,7},{7,6},{8,9},{9,8},{10,11... | collective-permute-start | bytes 1572872 | tf_op jit(solution)/shard_map/ppermute | solution.py:104
  445.4 192.7 %reduce-scatter.9.cloned.1.call-start = ((), (), s32[]{:S(2)}) async-start(), calls=%async_computation.9 | async-start | bytes 2228224 | tf_op jit(solution)/shard_map/reduce_scatter | solution.py:381
  451.8 60.0 %copy-start.51 = (f32[256]{0:T(256)S(1)}, f32[256]{0:T(256)}, u32[]{:S(2)}) copy-start(f32[256]{0:T(256)} %copy-done.50) | copy-start | bytes 3076
  451.8 13.5 %collective-permute-start.6 = (bf16[256,1024]{1,0:T(8,128)(2,1)}, bf16[256,1024]{1,0:T(8,128)(2,1)}, u32[]{:S(2)}, u32[]{:S(2)}) collective-permute-start(bf16[256,1024]{1,0:T(8,128)(2,1)} %constant_dynamic-slice_fusion), channel_id=1, source_target_pairs={{0,1},{1,0},{2,3},{3,2},{4,5},{5,4},{6,7},{7,6},{8,9},{9,8},{10,11... | collective-permute-start | bytes 1572872 | tf_op jit(solution)/shard_map/ppermute | solution.py:113
  467.3 170.9 %copy-start.46 = (f32[1,2,16,128]{3,1,2,0:T(2,128)S(1)}, f32[1,2,16,128]{3,1,2,0:T(2,128)}, u32[]{:S(2)}) copy-start(f32[1,2,16,128]{3,1,2,0:T(2,128)} %copy-done.45) | copy-start | bytes 49156
  515.5 249.5 %all-reduce.2.cloned.1.call-start = ((), (), s32[]{:S(2)}) async-start(), calls=%async_computation.13 | async-start | bytes 327680 | tf_op jit(solution)/shard_map/psum | solution.py:394
  517.5 318.2 %all-gather.12.cloned.1.call-start = ((), (), s32[]{:S(2)}) async-start(), calls=%async_computation.12 | async-start | bytes 2162688 | tf_op jit(solution)/shard_map/all_gather | solution.py:335
  573.0 295.9 %all-gather.10.cloned.1.call-start = ((), (), s32[]{:S(2)}) async-start(), calls=%async_computation.10 | async-start | bytes 2228224 | tf_op jit(solution)/shard_map/all_gather | solution.py:380
  649.9 26.7 %collective-permute-start.9 = (bf16[2,256,1024]{2,1,0:T(8,128)(2,1)}, bf16[2,256,1024]{2,1,0:T(8,128)(2,1)}, u32[]{:S(2)}, u32[]{:S(2)}) collective-permute-start(bf16[2,256,1024]{2,1,0:T(8,128)(2,1)} %split.29), channel_id=1, source_target_pairs={{0,1},{1,0},{2,3},{3,2},{4,5},{5,4},{6,7},{7,6},{8,9},{9,8},{10,11... | collective-permute-start | bytes 3145736 | tf_op jit(solution)/shard_map/ppermute | solution.py:113
  664.5 35.0 %collective-permute-start.8 = (bf16[2,1024,256]{2,1,0:T(8,128)(2,1)}, bf16[2,1024,256]{2,1,0:T(8,128)(2,1)}, u32[]{:S(2)}, u32[]{:S(2)}) collective-permute-start(bf16[2,1024,256]{2,1,0:T(8,128)(2,1)} %split.27), channel_id=1, source_target_pairs={{0,1},{1,0},{2,3},{3,2},{4,5},{5,4},{6,7},{7,6},{8,9},{9,8},{10,11... | collective-permute-start | bytes 3145736 | tf_op jit(solution)/shard_map/ppermute | solution.py:113
  675.2 44.0 %collective-permute-start.7 = (bf16[2,1024,256]{2,1,0:T(8,128)(2,1)S(1)}, bf16[2,1024,256]{2,1,0:T(8,128)(2,1)S(1)}, u32[]{:S(2)}, u32[]{:S(2)}) collective-permute-start(bf16[2,1024,256]{2,1,0:T(8,128)(2,1)S(1)} %split.25), channel_id=1, source_target_pairs={{0,1},{1,0},{2,3},{3,2},{4,5},{5,4},{6,7},{7,6},{8,9},{9,8},{10,11... | collective-permute-start | bytes 3145736 | tf_op jit(solution)/shard_map/ppermute | solution.py:113
  (52 other events, 812.4 us)
Sparse Core Ops, SparseCore 0:
  10.2 77.6 all-gather.7
  119.0 76.6 all-gather.5
  300.7 102.8 reduce-scatter.4
  407.5 104.2 reduce-scatter.6
  515.8 57.1 reduce-scatter.10
  577.6 60.5 reduce-scatter.8
  643.7 121.2 all-reduce.1
  767.8 58.5 all-gather.11
  828.6 40.2 all-gather.9
